TPU v7x, 256 devices: a whole 4x4x8 slice. The times are simulated.
256 devices in a mesh: dom: 32 (over y, x, z_lo), orient: 8 (over z_hi, core).
Axes of the slice: x: 4, y: 4, z: 8 (z_hi: 4, z_lo: 2; z = z_hi * 2 + z_lo), core: 2. Of those that a mesh axis runs over, the one named last changes fastest.
Arguments:
- particles: bfloat16 [8192, 16384], P('dom'), may hold values from -200 to 200
- refs: bfloat16 [64, 8, 16384], P('dom', 'orient'), may hold values from -6 to 6
- inv_sigma2: float32 [8192], replicated, may hold values from 0.0005 to 0.005
- offsets: int32 [9, 2], replicated, may hold values from -3 to 3, as said below
- owner_map: int32 [64], replicated, may hold values from 0 to 63, each once
- center: int32 [8192], P('dom'), may hold values from 0 to 7
Outputs:
- class_slices: float32 [64, 8, 16384], P('dom', 'orient')
- loglik: float32 [8192], P('dom')
Inputs may be any that keep to these rules, and one draw needn't show every extreme that they name: `offsets`: each of the 9 translations has x and y within the range; every value of the range occurs in each column.
All inputs are finite; a program needn't handle non-finite values.
Results may differ from a plain program's by a relative error of at most 0.013.
Values may be sent and summed in bfloat16 or wider, within the bound.
A program may use at most 128 MiB of HBM per device.

v0:
```python
import math

import jax
import jax.numpy as jnp
from jax import lax
from jax.sharding import PartitionSpec as P

BOX = 128
FREQS = 8192
FEAT = 16384


neg_fill = -1e30


def phase_tables(offsets):
    freq_index = jnp.arange(FREQS, dtype=jnp.int32)
    half_box = BOX // 2
    freq_x = freq_index % half_box
    freq_y = freq_index // half_box
    freq_y = jnp.where(freq_y < half_box, freq_y, freq_y - BOX)
    angle_table = (
        2.0
        * math.pi
        / BOX
        * (
            offsets[:, 0:1].astype(jnp.float32) * freq_x[None, :].astype(jnp.float32)
            + offsets[:, 1:2].astype(jnp.float32) * freq_y[None, :].astype(jnp.float32)
        )
    )
    return (jnp.cos(angle_table), jnp.sin(angle_table))


def shift_slices(slices_f32, inv_sigma2, cosine_table, sine_table):
    real_part = slices_f32[:, :FREQS] * inv_sigma2[None, :]
    imag_part = slices_f32[:, FREQS:] * inv_sigma2[None, :]
    cos_rows = cosine_table[:, None, :]
    sin_rows = sine_table[:, None, :]
    shifted_real = real_part[None] * cos_rows + imag_part[None] * sin_rows
    shifted_imag = imag_part[None] * cos_rows - real_part[None] * sin_rows
    return jnp.concatenate([shifted_real, shifted_imag], axis=2).astype(jnp.bfloat16)


def slice_power(slices_f32, inv_sigma2):
    real_part = slices_f32[:, :FREQS]
    imag_part = slices_f32[:, FREQS:]
    return 0.5 * jnp.sum(
        inv_sigma2[None, :] * (real_part * real_part + imag_part * imag_part), axis=1
    )


def rotate_back(sums, cosine_table, sine_table):
    real_part = sums[:, :, :FREQS]
    imag_part = sums[:, :, FREQS:]
    cos_rows = cosine_table[:, None, :]
    sin_rows = sine_table[:, None, :]
    out_real = jnp.sum(real_part * cos_rows - imag_part * sin_rows, axis=0)
    out_imag = jnp.sum(imag_part * cos_rows + real_part * sin_rows, axis=0)
    return jnp.concatenate([out_real, out_imag], axis=1)


def allowed_mask(orient_ids, center, orients):
    distance = jnp.abs(orient_ids[:, None] - center[None, :])
    circular = jnp.minimum(distance, orients - distance)
    return circular <= orients // 4


def per_device(particles, refs, inv_sigma2, offsets, owner_map, center):
    slot_dev = refs.shape[0]
    ori_dev = refs.shape[1]
    orients = ori_dev * lax.axis_size("orient")
    classes = slot_dev * lax.axis_size("dom")
    shifts = offsets.shape[0]
    part_rows = particles.shape[0]
    cosine_table, sine_table = phase_tables(offsets)
    orient_ids = lax.axis_index("orient") * ori_dev + jnp.arange(ori_dev, dtype=jnp.int32)
    allowed = allowed_mask(orient_ids, center, orients)
    shard_piece = lax.all_gather(refs, "dom", axis=0, tiled=True)
    pieces = shard_piece.shape[0]
    slices_f32 = shard_piece.reshape(pieces * ori_dev, FEAT).astype(jnp.float32)
    shifted = shift_slices(slices_f32, inv_sigma2, cosine_table, sine_table)
    powers = slice_power(slices_f32, inv_sigma2)
    scores = jnp.dot(
        shifted.reshape(shifts * pieces * ori_dev, FEAT),
        particles.T,
        preferred_element_type=jnp.float32,
    )
    log_like = scores.reshape(shifts, pieces, ori_dev, part_rows) - powers.reshape(
        1, pieces, ori_dev, 1
    )
    log_like = jnp.where(allowed[None, None], log_like, neg_fill)
    local_best = jnp.max(log_like, axis=(0, 1, 2))
    best_score = lax.pmax(local_best, "orient")
    expo = jnp.exp(log_like - best_score)
    weight_total = lax.psum(jnp.sum(expo, axis=(0, 1, 2)), "orient")
    weights = (expo / weight_total).astype(jnp.bfloat16)
    loglik = best_score + jnp.log(weight_total)
    by_class = jnp.take(weights, owner_map, axis=1)
    sums = jnp.dot(
        by_class.reshape(shifts * classes * ori_dev, part_rows),
        particles,
        preferred_element_type=jnp.float32,
    )
    sums = sums.reshape(shifts, classes * ori_dev, FEAT)
    full_terms = rotate_back(sums, cosine_table, sine_table).reshape(classes, ori_dev, FEAT)
    summed = lax.psum(full_terms, "dom")
    class_slices = lax.dynamic_slice_in_dim(summed, lax.axis_index("dom") * slot_dev, slot_dev, 0)
    return (class_slices, loglik)


def solution(mesh):
    return jax.shard_map(
        per_device,
        mesh=mesh,
        in_specs=(P("dom", None), P("dom", "orient", None), P(), P(), P(), P("dom")),
        out_specs=(P("dom", "orient", None), P("dom")),
        check_vma=False,
    )
```

profile of v0, /device:TPU:2, one launch (start us, length us, event | category | flops | bytes accessed | tf_op | source)
XLA Modules:
  0.0 621.7 jit_solution(2994139814048760225)
XLA Ops:
  7.2 0.0 copy-start
  7.2 0.0 all-gather.2.cloned.1.call-start
  7.2 1.6 copy.10
  8.8 0.0 all-gather.2.cloned.1.call-update
  8.8 0.0 all-reduce.2.cloned.1.call-start
  8.9 0.7 compare_select_fusion.1
  9.6 0.7 compare_and_fusion
  10.2 0.7 fusion.28
  10.9 0.8 convert_bitcast_fusion.1
  11.7 1.9 fusion.18
  13.6 163.8 %all-gather.2.cloned.1.call-done = bf16[64,1,16384]{2,1,0:T(2,128)(2,1)} async-done(((bf16[2,1,16384]{2,1,0:T(2,128)(2,1)}), bf16[64,1,16384]{2,1,0:T(2,128)(2,1)}) %all-gather.2.cloned.1.call-update) | async-done | bytes 2097168 | tf_op jit(solution)/shard_map/all_gather | solution.py:78
  177.4 4.6 copy.17
  182.0 0.0 copy-done
  182.0 0.6 multiply_reduce_fusion
  182.6 8.6 %add_convert_fusion = (bf16[9,64,8192]{2,1,0:T(8,128)(2,1)}, bf16[9,64,8192]{2,1,0:T(8,128)(2,1)}) fusion(f32[9,8192]{1,0:T(8,128)S(1)} %get-tuple-element.10, f32[64,8192]{1,0:T(8,128)S(1)} %get-tuple-element.7, f32[9,8192]{1,0:T(8,128)S(1)} %get-tuple-element.9, f32[64,8192]{1,0:T(8,128)S(1)} %get-tuple-element.8), kind=kLoop, calls=%fused_computation.8 | loop fusion | flops 37748736 | bytes 23658496 | tf_op jit(solution)/shard_map/convert.1
  191.2 14.1 %fusion.30 = (f32[256]{0:T(256)S(1)}, f32[9,64,256]{2,1,0:T(8,128)S(1)}) fusion(f32[64]{0:T(128)S(1)} %broadcast_multiply_fusion, bf16[256,16384]{1,0:T(8,128)(2,1)} %param.6, bf16[9,64,8192]{2,1,0:T(8,128)(2,1)} %get-tuple-element.5, bf16[9,64,8192]{2,1,0:T(8,128)(2,1)} %get-tuple-element.4, pred[256]{0:T(512)(128)(4,1)S(1)} %fusion.28), kind=kOutput, calls=%fused_computation.51 | convolution fusion | flops 4870029312 | bytes 27854336 | tf_op jit(solution)/shard_map/dot_general | solution.py:83
  205.3 14.2 %pmax.7 = f32[256]{0:T(256)S(1)} all-reduce(f32[256]{0:T(256)S(1)} %get-tuple-element.13), channel_id=1, replica_groups=mesh['dom'=32,'orient'=8] {'orient'}, use_global_device_ids=true, to_apply=%region_2.3 | all-reduce | flops 256 | bytes 2048 | tf_op jit(solution)/shard_map/pmax | solution.py:93
  219.5 0.1 fusion.19
  219.7 14.9 %psum.14 = f32[256]{0:T(256)S(1)} all-reduce(f32[256]{0:T(256)S(1)} %fusion.19), channel_id=1, replica_groups=mesh['dom'=32,'orient'=8] {'orient'}, use_global_device_ids=true, to_apply=%region_4.5 | all-reduce | flops 256 | bytes 2048 | tf_op jit(solution)/shard_map/psum | solution.py:95
  234.6 0.1 divide_convert_fusion
  234.7 0.2 copy.11
  234.9 0.6 gather_fusion
  235.5 0.1 select_bitcast_fusion
  235.7 18.1 %fusion.4 = f32[9,64,16384]{2,1,0:T(8,128)} fusion(bf16[256,16384]{1,0:T(8,128)(2,1)} %param.6, bf16[9,64,256]{2,0,1:T(8,128)(2,1)S(1)} %select_bitcast_fusion), kind=kOutput, calls=%fused_computation.9 | convolution fusion | flops 4831838208 | bytes 46432256 | tf_op jit(solution)/shard_map/dot_general | solution.py:99
  253.8 13.8 %subtract_reduce_fusion = (f32[64,8192]{1,0:T(8,128)S(1)}, f32[64,8192]{1,0:T(8,128)S(1)}) fusion(f32[9,64,16384]{2,1,0:T(8,128)} %fusion.4, f32[9,8192]{1,0:T(8,128)S(1)} %get-tuple-element.10, f32[9,8192]{1,0:T(8,128)S(1)} %get-tuple-element.9), kind=kLoop, calls=%fused_computation.6 | loop fusion | flops 36700160 | bytes 42532864 | tf_op jit(solution)/shard_map/reduce_sum | solution.py:57
  267.6 0.3 pad_maximum_fusion
  267.9 4.0 reshape.200
  271.9 0.0 all-reduce.2.cloned.1.call-update
  271.9 0.6 log_add_fusion
  272.5 340.7 %all-reduce.2.cloned.1.call-done = f32[64,1,16384]{2,1,0:T(1,128)} async-done(((f32[64,1,16384]{2,1,0:T(1,128)}), f32[64,1,16384]{2,1,0:T(1,128)}) %all-reduce.2.cloned.1.call-update) | async-done | bytes 4194320 | tf_op jit(solution)/shard_map/psum | solution.py:106
  613.3 1.6 constant_dynamic-slice_fusion
  (3 shorter events, 0.0 us)
Async XLA Ops:
  7.2 174.8 %copy-start = (f32[8192]{0:T(1024)S(1)}, f32[8192]{0:T(1024)}, u32[]{:S(2)}) copy-start(f32[8192]{0:T(1024)} %param.8) | copy-start | bytes 98308
  7.2 170.2 %all-gather.2.cloned.1.call-start = ((), (), s32[]{:S(2)}) async-start(), calls=%async_computation | async-start | bytes 4325376 | tf_op jit(solution)/shard_map/all_gather | solution.py:78
  8.8 604.4 %all-reduce.2.cloned.1.call-start = ((), (), s32[]{:S(2)}) async-start(), calls=%async_computation.1 | async-start | bytes 8388608 | tf_op jit(solution)/shard_map/psum | solution.py:106
Sparse Core Ops, SparseCore 0:
  10.4 166.9 all-gather.1
  272.1 341.1 all-reduce.1
where the time goes:
time: 625 us; the launch traced here: 622 us
  waiting for transfers between devices  505 us (81%)
  matrix products  32.2 us (5%)
  blocking collectives  29.2 us (5%)
  other arithmetic  29.1 us (5%)
  between operations  14.1 us (2%)
  local copies, waits for them, and re-layouts  12.5 us (2%)
    psum x1, waiting for transfers between devices, per_device(): summed = lax.psum(full_terms, 'dom')  341 us
    all_gather x1, waiting for transfers between devices, per_device(): shard_piece = lax.all_gather(refs, 'dom', axis=0, tiled=True)  164 us
    dot_general x1, matrix products, per_device(): jnp.dot(by_class.reshape(shifts * classes * ori_dev, part_rows), particle...  18.1 us
    psum x1, blocking collectives, per_device(): weight_total = lax.psum(jnp.sum(expo, axis=(0, 1, 2)), 'orient')  14.9 us
    pmax x1, blocking collectives, per_device(): best_score = lax.pmax(local_best, 'orient')  14.2 us
    dot_general x1, matrix products, per_device(): jnp.dot(shifted.reshape(shifts * pieces * ori_dev, FEAT), particles.T, pr...  14.1 us
    reduce_sum x1, other arithmetic, rotate_back(): out_real = jnp.sum(real_part * cos_rows - imag_part * sin_rows, axis=0)  13.8 us
  transfers between devices with their start and end apart: 2, of which 2 were waited for; matrix products, arithmetic and copies ran while one was open for 1% of the time, Pallas kernels for 0%

commit v1 on v0

v1 whole, which is shorter than its diff:
```python
import functools
import math

import jax
import jax.numpy as jnp
from jax import lax
from jax.experimental import pallas as pl
from jax.experimental.pallas import tpu as pltpu
from jax.sharding import PartitionSpec as P

BOX = 128
CHUNKS = 4
GROUPS = 4
RING = 4
NEG_FILL = -1e30
MESH = pl.DeviceIdType.MESH
BF16, F32 = jnp.bfloat16, jnp.float32


def unit_circle(phase):
    folded = ((phase + 64) & 127) - 64
    quarter = (folded + 16) >> 5
    x = (folded - quarter * 32).astype(F32) * (2.0 * math.pi / BOX)
    x2 = x * x
    sine = x * (1.0 + x2 * (-1 / 6 + x2 * (1 / 120 + x2 * (-1 / 5040 + x2 * (1 / 362880)))))
    cosine = 1.0 + x2 * (-0.5 + x2 * (1 / 24 + x2 * (-1 / 720 + x2 * (1 / 40320))))
    odd = (quarter & 1) == 1
    cos_sign = jnp.where(((quarter + 1) & 2) == 2, -1.0, 1.0)
    sin_sign = jnp.where((quarter & 2) == 2, -1.0, 1.0)
    return jnp.where(odd, sine, cosine) * cos_sign, jnp.where(odd, cosine, sine) * sin_sign


def em_kernel(
    n_dom, n_ori, shifts,
    refs_ref, part_hbm, inv_hbm, off_ref, omap_hbm, center_hbm,
    out_ref, loglik_ref,
    part, stage, mine, gath, rows, perm, perm_t, cos_tab, sin_tab, lhs, acc, prods, power, inv_ref, omap_ref, center_ref,
    stat_out, stat_in, by_class, sends, far_in, near_in, send2, recv2,
    part_sem, small_sem, ag_send, ag_recv, st_send, st_recv, rs_send, far_sem, early_sem, late_sem, rs_recv,
):
    freqs = inv_ref.shape[1]
    slots = 2 * n_dom
    lanes = mine.shape[2]
    width = freqs // CHUNKS
    half = RING
    me = lax.axis_index("dom")
    my_ori = lax.axis_index("orient")
    my_y, my_x, my_z = me // 8, (me // 2) % 4, me % 2

    def axes(c):
        odd = c % 2
        return odd, my_y * (1 - odd) + my_x * odd, my_x * (1 - odd) + my_y * odd

    def device(odd, v, u, z):
        return {"dom": ((v * (1 - odd) + u * odd) * 4 + u * (1 - odd) + v * odd) * 2 + z}

    def step(a, by):
        return (a + by) % RING

    def tile_row(odd, h, k):
        return pl.multiple_of((32 * h + 8 * k) * (1 - odd) + (16 * k + 8 * h) * odd, 8)

    def send(src, dst, send_sem, recv_sem, to):
        pltpu.make_async_remote_copy(
            src_ref=src, dst_ref=dst, send_sem=send_sem, recv_sem=recv_sem, device_id=to, device_id_type=MESH
        ).start()

    def wait(ref, sem):
        pltpu.make_async_copy(ref, ref, sem).wait()

    smalls = [
        pltpu.make_async_copy(src, dst, small_sem.at[k])
        for k, (src, dst) in enumerate(((inv_hbm, inv_ref), (omap_hbm, omap_ref), (center_hbm, center_ref)))
    ]

    def part_copies(k):
        return [
            pltpu.make_async_copy(
                part_hbm.at[:, pl.ds(pl.multiple_of(base + k * lanes, lanes), lanes)],
                part.at[:, pl.ds(pl.multiple_of((2 * k + r) * lanes, lanes), lanes)],
                part_sem.at[k // GROUPS],
            )
            for r, base in enumerate((0, freqs))
        ]

    for copy in smalls:
        copy.start()

    barrier = pltpu.get_barrier_semaphore()

    def greet(to):
        pl.semaphore_signal(barrier, inc=1, device_id=to, device_id_type=MESH)

    peers = [device(0, my_y, my_x, 1 - my_z)]
    for by in (1, 2, 3):
        for z in (my_z, 1 - my_z):
            peers.append(device(0, my_y, step(my_x, by), z))
            peers.append(device(0, step(my_y, by), my_x, z))
    for to in peers:
        greet(to)

    def greet_ori(i, carry):
        greet({"orient": lax.rem(my_ori + i, n_ori)})
        return carry

    lax.fori_loop(1, n_ori, greet_ori, 0)

    def exchange(first, second):
        for odd in range(2):
            there = lax.broadcasted_iota(jnp.int32, (256, 256), 0)
            here = lax.broadcasted_iota(jnp.int32, (256, 256), 1)
            for ref, out, src in ((first, there, here), (second, here, there)):
                at, s, q = src >> 4, (src >> 3) & 1, src & 7
                if odd:
                    row = ((at >> 1) & 3) * 8 + (at >> 3) * 4 + (at & 1) * 2 + s
                else:
                    row = at * 2 + s
                ref[odd] = (out == q * 32 + row).astype(F32).astype(BF16)

    for c in range(CHUNKS):
        for r in range(2):
            for g in range(GROUPS):
                for j in range(lanes // 128):
                    at = r * freqs + c * width + g * lanes + j * 128
                    stage[j, pl.ds(c * 16 + r * GROUPS + g, 2, stride=8), :] = refs_ref[:, pl.ds(at, 128)].astype(F32)
        for j in range(lanes // 128):
            mine[c, :, pl.ds(j * 128, 128)] = stage[j, pl.ds(c * 16, 16), :].astype(BF16)

    pl.semaphore_wait(barrier, len(peers) + n_ori - 1)

    def gather0(c, carry):
        odd, v, u = axes(c)
        at = v * 8 + u * 2 + my_z
        send(mine.at[c], gath.at[c, at], ag_send.at[c], ag_recv.at[c, 0], device(odd, v, u, 1 - my_z))
        gath[c, at] = mine[c]
        return carry

    def gather1(c):
        odd, v, u = axes(c)
        wait(mine.at[c], ag_recv.at[c, 0])
        pair = gath.at[c, pl.ds(v * 8 + u * 2, 2)]
        send(pair, pair, ag_send.at[c], ag_recv.at[c, 1], device(odd, v, step(u, 1), my_z))
        send(pair, pair, ag_send.at[c], ag_recv.at[c, 2], device(odd, v, step(u, 3), my_z))

    def gather2(c):
        odd, v, u = axes(c)
        for k, by in ((0, 1), (1, 3)):
            came = v * 8 + step(u, 4 - by) * 2
            wait(gath.at[c, pl.ds(came, 2)], ag_recv.at[c, 1 + k])
            one = gath.at[c, came + k]
            send(one, one, ag_send.at[c], ag_recv.at[c, 3 + k], device(odd, v, step(u, by), my_z))

    def gather3(c):
        odd, v, u = axes(c)
        for k in range(2):
            wait(gath.at[c, v * 8 + step(u, 2) * 2 + k], ag_recv.at[c, 3 + k])
        block = gath.at[c, pl.ds(v * 8, 8)]
        send(block, block, ag_send.at[c], ag_recv.at[c, 5], device(odd, step(v, 1), u, my_z))
        send(block, block, ag_send.at[c], ag_recv.at[c, 6], device(odd, step(v, 3), u, my_z))

    def gather4(c):
        odd, v, u = axes(c)
        for k, by in ((0, 1), (1, 3)):
            came = step(v, 4 - by) * 8
            wait(gath.at[c, pl.ds(came, 8)], ag_recv.at[c, 5 + k])
            part_of = gath.at[c, pl.ds(came + k * half, half)]
            send(part_of, part_of, ag_send.at[c], ag_recv.at[c, 7 + k], device(odd, step(v, by), u, my_z))

    def gather5(c):
        odd, v, u = axes(c)
        for k in range(2):
            wait(gath.at[c, pl.ds(step(v, 2) * 8 + k * half, half)], ag_recv.at[c, 7 + k])

    def pair(k, stage):
        def one(i, carry):
            stage(2 * k + i)
            return carry

        lax.fori_loop(0, 2, one, 0)

    lax.fori_loop(0, CHUNKS, gather0, 0)

    def fetch(k, carry):
        for copy in part_copies(k):
            copy.start()
        return carry

    lax.fori_loop(0, CHUNKS * GROUPS, fetch, 0)
    pair(0, gather1)
    exchange(perm, perm_t)

    shift_ids = lax.broadcasted_iota(jnp.int32, (shifts, 128), 0)
    off_x = jnp.zeros((shifts, 128), jnp.int32)
    off_y = jnp.zeros((shifts, 128), jnp.int32)
    for t in range(shifts):
        off_x = jnp.where(shift_ids == t, off_ref[0, t], off_x)
        off_y = jnp.where(shift_ids == t, off_ref[1, t], off_y)

    def tables(j, carry):
        for h in range(4):
            at = pl.multiple_of(j * 512 + h * 128, 128)
            freq = lax.broadcasted_iota(jnp.int32, (shifts, 128), 1) + at
            fx = freq & (BOX // 2 - 1)
            fy = freq >> 6
            fy = jnp.where(fy < BOX // 2, fy, fy - BOX)
            cosine, sine = unit_circle(off_x * fx + off_y * fy)
            cos_tab[:, pl.ds(at, 128)] = cosine
            sin_tab[:, pl.ds(at, 128)] = sine
        return carry

    lax.fori_loop(0, freqs // 1024, tables, 0)
    pair(0, gather2)
    pair(1, gather1)
    lax.fori_loop(freqs // 1024, freqs // 512, tables, 0)
    pair(0, gather3)
    pair(1, gather2)
    for copy in smalls:
        copy.wait()
    acc[...] = jnp.zeros_like(acc)
    power[...] = jnp.zeros_like(power)
    pair(0, gather4)
    pair(1, gather3)

    def score_chunk(c, carry):
        odd, v, u = axes(c)
        wait(part.at[:, pl.ds(0, 2 * width)], part_sem.at[c])
        gather5(c)

        for h in range(2):
            spread = jnp.dot(
                perm[odd], gath[c, pl.ds(16 * h, 16)].reshape(256, lanes), preferred_element_type=F32
            )
            for q in range(8):
                for k in range(4):
                    rows[q, pl.ds(tile_row(odd, h, k), 8), :] = spread[q * 32 + k * 8:q * 32 + k * 8 + 8, :]

        for g in range(GROUPS):
            base = pl.multiple_of(c * width + g * lanes, lanes)
            for j in range(lanes // 128):
                at = pl.ds(j * 128, 128)
                there = pl.ds(pl.multiple_of(base + j * 128, 128), 128)
                real = rows[g, :, at]
                imag = rows[GROUPS + g, :, at]
                inv = inv_ref[:, there]
                re = real * inv
                im = imag * inv
                power[...] += re * real + im * imag
                for t in range(shifts):
                    cosine = cos_tab[pl.ds(t, 1), there]
                    sine = sin_tab[pl.ds(t, 1), there]
                    into = lhs.at[g % 2, pl.ds(t * slots, slots)]
                    into[:, at] = (re * cosine + im * sine).astype(BF16)
                    into[:, pl.ds(lanes + j * 128, 128)] = (im * cosine - re * sine).astype(BF16)
            acc[...] += lax.dot_general(
                lhs[g % 2], part[:, pl.ds(pl.multiple_of(2 * base, 2 * lanes), 2 * lanes)],
                (((1,), (1,)), ((), ())), preferred_element_type=F32,
            )

        for k in range(CHUNKS // 2):
            @pl.when(c == k)
            def _():
                gather4(CHUNKS // 2 + k)

        return carry

    lax.fori_loop(0, CHUNKS, score_chunk, 0)

    power_col = 0.5 * jnp.sum(power[...], axis=1, keepdims=True)
    distance = jnp.abs(my_ori - center_ref[...])
    allowed = jnp.minimum(distance, n_ori - distance) <= n_ori // 4
    best = None
    for t in range(shifts):
        at = pl.ds(t * slots, slots)
        value = jnp.where(allowed, acc[at, :] - power_col, NEG_FILL)
        acc[at, :] = value
        top = jnp.max(value, axis=0, keepdims=True)
        best = top if best is None else jnp.maximum(best, top)
    total = jnp.zeros_like(best)
    for t in range(shifts):
        total += jnp.sum(jnp.exp(acc[pl.ds(t * slots, slots), :] - best), axis=0, keepdims=True)
    stat_out[0:1, :] = best
    stat_out[1:2, :] = total

    def stat_send(i, carry):
        send(stat_out, stat_in.at[my_ori], st_send, st_recv, {"orient": lax.rem(my_ori + i, n_ori)})
        return carry

    lax.fori_loop(1, n_ori, stat_send, 0)
    stat_in[my_ori] = stat_out[...]
    if n_ori > 1:
        others = stat_in.at[pl.ds(0, n_ori - 1)]
        wait(others, st_recv)
        wait(others, st_send)
    bests = [stat_in[o, 0:1, :] for o in range(n_ori)]
    best = functools.reduce(jnp.maximum, bests)
    total = sum(stat_in[o, 1:2, :] * jnp.exp(bests[o] - best) for o in range(n_ori))
    loglik_ref[...] = best + jnp.log(total)

    pick = (lax.broadcasted_iota(jnp.int32, (slots, slots), 0) == omap_ref[...]).astype(F32).astype(BF16)
    weights = jnp.concatenate(
        [(jnp.exp(acc[pl.ds(t * slots, slots), :] - best) / total).astype(BF16) for t in range(shifts)], axis=1
    )
    picked = lax.dot_general(pick, weights, (((0,), (0,)), ((), ())), preferred_element_type=F32).astype(BF16)
    pcount = acc.shape[1]
    for t in range(shifts):
        by_class[pl.ds(t * slots, slots), :] = picked[:, t * pcount:(t + 1) * pcount]

    def sum_chunk(c):
        odd, v, u = axes(c)

        def multiply(g):
            base = pl.multiple_of(2 * (c * width + g * lanes), 2 * lanes)
            prods[g % 2] = jnp.dot(by_class[...], part[:, pl.ds(base, 2 * lanes)], preferred_element_type=F32)

        multiply(0)
        for g in range(GROUPS):
            if g + 1 < GROUPS:
                multiply(g + 1)
            for j in range(lanes // 128):
                at = pl.ds(j * 128, 128)
                there = pl.ds(pl.multiple_of(c * width + g * lanes + j * 128, 128), 128)
                out_real = out_imag = None
                for t in range(shifts):
                    cosine = cos_tab[pl.ds(t, 1), there]
                    sine = sin_tab[pl.ds(t, 1), there]
                    re = prods[g % 2, pl.ds(t * slots, slots), at]
                    im = prods[g % 2, pl.ds(t * slots, slots), pl.ds(lanes + j * 128, 128)]
                    term_real = re * cosine - im * sine
                    term_imag = im * cosine + re * sine
                    out_real = term_real if t == 0 else out_real + term_real
                    out_imag = term_imag if t == 0 else out_imag + term_imag
                rows[g, :, at] = out_real
                rows[GROUPS + g, :, at] = out_imag

        for h in range(2):
            tiles = [rows[q, pl.ds(tile_row(odd, h, k), 8), :] for q in range(8) for k in range(4)]
            spread = jnp.dot(
                perm_t[odd], jnp.concatenate(tiles, axis=0).astype(BF16), preferred_element_type=F32
            ).astype(BF16)
            sends[c, pl.ds(16 * h, 16)] = spread.reshape(16, 16, lanes)

    def reduce0(c):
        odd, v, u = axes(c)
        for k, by in ((0, 1), (1, 3)):
            to = device(odd, step(v, by), u, my_z)
            send(sends.at[c, pl.ds(step(v, 2) * 8 + k * half, half)], far_in.at[c, k], rs_send.at[c], far_sem.at[c, k], to)
        for k, by in ((0, 1), (1, 3)):
            to = device(odd, step(v, by), u, my_z)
            other = (1 - k) * half
            send(
                sends.at[c, pl.ds(step(v, by) * 8 + other, half)], near_in.at[c, k, pl.ds(other, half)],
                rs_send.at[c], early_sem.at[c, k], to,
            )

    def reduce1(c):
        odd, v, u = axes(c)
        for k, by in ((0, 1), (1, 3)):
            wait(far_in.at[c, k], far_sem.at[c, k])
            at = step(v, by) * 8 + k * half

            def add(i, carry):
                sends[c, at + i] = (sends[c, at + i].astype(F32) + far_in[c, k, i].astype(F32)).astype(BF16)
                return carry

            lax.fori_loop(0, half, add, 0)
            send(
                sends.at[c, pl.ds(at, half)], near_in.at[c, k, pl.ds(k * half, half)], rs_send.at[c],
                late_sem.at[c, k], device(odd, step(v, by), u, my_z),
            )

    def reduce2(c):
        odd, v, u = axes(c)
        for k in range(2):
            wait(near_in.at[c, k, pl.ds((1 - k) * half, half)], early_sem.at[c, k])
            wait(near_in.at[c, k, pl.ds(k * half, half)], late_sem.at[c, k])

        def add(q, carry):
            send2[c, q] = (
                sends[c, v * 8 + q].astype(F32) + near_in[c, 0, q].astype(F32) + near_in[c, 1, q].astype(F32)
            ).astype(BF16)
            return carry

        lax.fori_loop(0, 8, add, 0)
        home = u * 2 + my_z

        def share(i, carry):
            q = (home + i) % 8
            send(send2.at[c, q], recv2.at[c, home], rs_send.at[c], rs_recv.at[c], device(odd, v, q // 2, q % 2))
            return carry

        lax.fori_loop(1, 8, share, 0)
        recv2[c, home] = send2[c, home]

    def sum_step(i, carry):
        @pl.when(i < CHUNKS)
        def _():
            sum_chunk(i)
            reduce0(i)

        @pl.when((i >= 1) & (i < CHUNKS + 1))
        def _():
            reduce1(i - 1)

        @pl.when(i >= 2)
        def _():
            reduce2(i - 2)

        return carry

    lax.fori_loop(0, CHUNKS + 2, sum_step, 0)

    for c in range(CHUNKS):
        wait(recv2.at[c, pl.ds(0, 7)], rs_recv.at[c])
        for j in range(lanes // 128):
            total = recv2[c, 0, :, pl.ds(j * 128, 128)].astype(F32)
            for q in range(1, 8):
                total += recv2[c, q, :, pl.ds(j * 128, 128)].astype(F32)
            for s in range(2):
                for r in range(2):
                    for g in range(GROUPS):
                        row = s * 8 + r * GROUPS + g
                        at = r * freqs + c * width + g * lanes + j * 128
                        out_ref[s, :, pl.ds(at, 128)] = total[row:row + 1, :]

    def drain(c, carry):
        wait(gath.at[c, pl.ds(0, n_dom - 1)], ag_send.at[c])
        wait(gath.at[c, pl.ds(0, 31)], rs_send.at[c])
        return carry

    lax.fori_loop(0, CHUNKS, drain, 0)


def per_device(n_dom, n_ori, particles, refs, inv_sigma2, offsets, owner_map, center):
    pcount, feat = particles.shape
    freqs = feat // 2
    shifts = offsets.shape[0]
    slots = 2 * n_dom
    lanes = freqs // (CHUNKS * GROUPS)
    vmem = pl.BlockSpec(memory_space=pltpu.VMEM)
    anywhere = pl.BlockSpec(memory_space=pl.ANY)
    dma = pltpu.SemaphoreType.DMA
    sums, loglik = pl.pallas_call(
        functools.partial(em_kernel, n_dom, n_ori, shifts),
        out_shape=(
            jax.ShapeDtypeStruct((2, 1, feat), F32),
            jax.ShapeDtypeStruct((1, pcount), F32),
        ),
        in_specs=[vmem, anywhere, anywhere, pl.BlockSpec(memory_space=pltpu.SMEM), anywhere, anywhere],
        out_specs=(vmem, vmem),
        scratch_shapes=[
            pltpu.VMEM((pcount, feat), BF16),
            pltpu.VMEM((lanes // 128, 16 * CHUNKS, 128), F32),
            pltpu.VMEM((CHUNKS, 16, lanes), BF16),
            pltpu.VMEM((CHUNKS, n_dom, 16, lanes), BF16),
            pltpu.VMEM((2 * GROUPS, slots, lanes), F32),
            pltpu.VMEM((2, 256, 256), BF16),
            pltpu.VMEM((2, 256, 256), BF16),
            pltpu.VMEM((shifts, freqs), F32),
            pltpu.VMEM((shifts, freqs), F32),
            pltpu.VMEM((2, shifts * slots, 2 * lanes), BF16),
            pltpu.VMEM((shifts * slots, pcount), F32),
            pltpu.VMEM((2, shifts * slots, 2 * lanes), F32),
            pltpu.VMEM((slots, 128), F32),
            pltpu.VMEM((1, freqs), F32),
            pltpu.VMEM((1, slots), jnp.int32),
            pltpu.VMEM((1, pcount), jnp.int32),
            pltpu.VMEM((8, pcount), F32),
            pltpu.VMEM((n_ori, 8, pcount), F32),
            pltpu.VMEM((shifts * slots, pcount), BF16),
            pltpu.VMEM((CHUNKS, n_dom, 16, lanes), BF16),
            pltpu.VMEM((CHUNKS, 2, RING, 16, lanes), BF16),
            pltpu.VMEM((CHUNKS, 2, 8, 16, lanes), BF16),
            pltpu.VMEM((CHUNKS, 8, 16, lanes), BF16),
            pltpu.VMEM((CHUNKS, 8, 16, lanes), BF16),
            dma((CHUNKS,)),
            dma((3,)),
            dma((CHUNKS,)),
            dma((CHUNKS, 9)),
            dma,
            dma,
            dma((CHUNKS,)),
            dma((CHUNKS, 2)),
            dma((CHUNKS, 2)),
            dma((CHUNKS, 2)),
            dma((CHUNKS,)),
        ],
        compiler_params=pltpu.CompilerParams(
            collective_id=0, has_side_effects=True, vmem_limit_bytes=56 * 1024 * 1024
        ),
        cost_estimate=pl.CostEstimate(
            flops=4 * shifts * slots * pcount * feat, bytes_accessed=2 * pcount * feat, transcendentals=0
        ),
    )(
        refs.reshape(2, feat), particles, inv_sigma2.reshape(1, freqs), offsets.T, owner_map.reshape(1, slots),
        center.reshape(1, pcount),
    )
    return sums, loglik.reshape(pcount)


def solution(mesh):
    return jax.shard_map(
        functools.partial(per_device, mesh.shape["dom"], mesh.shape["orient"]),
        mesh=mesh,
        in_specs=(P("dom", None), P("dom", "orient", None), P(), P(), P(), P("dom")),
        out_specs=(P("dom", "orient", None), P("dom")),
        check_vma=False,
    )
```

time: 625 us -> 77.9 us (0.12)
  waiting for transfers between devices: 505 us -> 0 us
  Pallas kernels: 0 us -> 73.5 us
  matrix products: 32.2 us -> 0 us
  blocking collectives: 29.2 us -> 0 us
  other arithmetic: 29.1 us -> 0 us
  between operations: 14.1 us -> 0.64 us
  local copies, waits for them, and re-layouts: 12.5 us -> 2.8 us
    psum x1 -> x0, waiting for transfers between devices: 341 us -> none  [per_device(): summed = lax.psum(full_terms, 'dom')]
    all_gather x1 -> x0, waiting for transfers between devices: 164 us -> none  [per_device(): shard_piece = lax.all_gather(refs, 'dom', axis=0, tiled=True)]
    pallas_call x0 -> x1, Pallas kernels: none -> 73.5 us  [per_device(): pl.pallas_call(functools.partial(em_kernel, n_dom, n_ori, shifts), out_sh...]
    dot_general x2 -> x0, matrix products: 32.2 us -> none  [the longest x1 18.1 us: per_device(): jnp.dot(by_class.reshape(shifts * classes * ori_dev, part_rows), particle...]
    psum x1 -> x0, blocking collectives: 14.9 us -> none  [per_device(): weight_total = lax.psum(jnp.sum(expo, axis=(0, 1, 2)), 'orient')]
    reduce_sum x3 -> x0, other arithmetic: 14.6 us -> none  [the longest x1 13.8 us: rotate_back(): out_real = jnp.sum(real_part * cos_rows - imag_part * sin_rows, axis=0)]
    pmax x1 -> x0, blocking collectives: 14.2 us -> none  [per_device(): best_score = lax.pmax(local_best, 'orient')]
    another operation x1 -> x0, other arithmetic: 8.62 us -> none
  transfers between devices with their start and end apart: 2 -> 0, of which waited for: 2 -> 0; matrix products, arithmetic and copies ran while one was open for 1% -> 0% of each run, Pallas kernels for 0% -> 0%
where the time goes in v1:
time: 77.9 us; the launch traced here: 76.9 us
  Pallas kernels  73.5 us (94%)
  local copies, waits for them, and re-layouts  2.8 us (4%)
    pallas_call x1, Pallas kernels, per_device(): pl.pallas_call(functools.partial(em_kernel, n_dom, n_ori, shifts), out_sh...  73.5 us
    unnamed x2, local copies, waits for them, and re-layouts  2.8 us

profile of v1, /device:TPU:2, one launch (start us, length us, event | category | flops | bytes accessed | tf_op | source)
XLA Modules:
  0.0 76.9 jit_solution(2795755029976552812)
XLA Ops:
  0.6 73.5 %shard_map.77 = (f32[2,1,16384]{2,1,0:T(1,128)}, f32[1,256]{1,0:T(1,128)}) custom-call(bf16[2,16384]{1,0:T(2,128)(2,1)} %bitcast.7, bf16[256,16384]{1,0:T(8,128)(2,1)} %part_hbm.1, f32[1,8192]{1,0:T(1,128)} %bitcast.8, s32[2,9]{1,0:T(2,128)} %bitcast.9, s32[1,64]{1,0:T(1,128)} %bitcast.11, s32[1,256]{1,0:T(1,128)} %bitcast.10), custom_call_target="tpu_custom_call" | custom-call | flops 9663676416 | bytes 8388608 | tf_op jit(solution)/shard_map/pallas_call | solution.py:442
  74.1 1.6 %copy.10 = f32[2,1,16384]{2,1,0:T(1,128)} copy(f32[2,1,16384]{2,1,0:T(1,128)} %get-tuple-element.8) | data formatting | bytes 262144
  75.7 1.2 %copy.11 = f32[256]{0:T(256)} copy(f32[256]{0:T(256)} %bitcast.6) | data formatting | bytes 2048

commit v2 on v1

--- a/solution.py
+++ b/solution.py
@@ -9,8 +9,10 @@
 from jax.sharding import PartitionSpec as P
 
 BOX = 128
-CHUNKS = 4
+CHUNKS = 8
 GROUPS = 4
+PAIRS = CHUNKS // 2
+LAG = CHUNKS // 4
 RING = 4
 NEG_FILL = -1e30
 MESH = pl.DeviceIdType.MESH
@@ -32,11 +34,11 @@
 
 def em_kernel(
     n_dom, n_ori, shifts,
-    refs_ref, part_hbm, inv_hbm, off_ref, omap_hbm, center_hbm,
+    refs_hbm, part_hbm, inv_hbm, off_hbm, omap_hbm, center_hbm,
     out_ref, loglik_ref,
-    part, stage, mine, gath, rows, perm, perm_t, cos_tab, sin_tab, lhs, acc, prods, power, inv_ref, omap_ref, center_ref,
+    part, stage, mine, gath, rows, perm, perm_t, cos_tab, sin_tab, lhs, acc, prods, power, refs_ref, off_ref, inv_ref, omap_ref, center_ref,
     stat_out, stat_in, by_class, sends, far_in, near_in, send2, recv2,
-    part_sem, small_sem, ag_send, ag_recv, st_send, st_recv, rs_send, far_sem, early_sem, late_sem, rs_recv,
+    part_sem, small_sem, ag_send, ag_recv, ag_near, ag_far, st_send, st_recv, rs_send, far_sem, early_sem, late_sem, rs_recv,
 ):
     freqs = inv_ref.shape[1]
     slots = 2 * n_dom
@@ -70,18 +72,19 @@
 
     smalls = [
         pltpu.make_async_copy(src, dst, small_sem.at[k])
-        for k, (src, dst) in enumerate(((inv_hbm, inv_ref), (omap_hbm, omap_ref), (center_hbm, center_ref)))
+        for k, (src, dst) in enumerate((
+            (refs_hbm, refs_ref), (off_hbm, off_ref), (inv_hbm, inv_ref), (omap_hbm, omap_ref), (center_hbm, center_ref)
+        ))
     ]
 
-    def part_copies(k):
-        return [
+    def fetch(k, carry):
+        for r, base in enumerate((0, freqs)):
             pltpu.make_async_copy(
-                part_hbm.at[:, pl.ds(pl.multiple_of(base + k * lanes, lanes), lanes)],
-                part.at[:, pl.ds(pl.multiple_of((2 * k + r) * lanes, lanes), lanes)],
-                part_sem.at[k // GROUPS],
-            )
-            for r, base in enumerate((0, freqs))
-        ]
+                part_hbm.at[:, pl.ds(pl.multiple_of(base + k * 2 * lanes, 2 * lanes), 2 * lanes)],
+                part.at[:, pl.ds(pl.multiple_of((2 * k + r) * 2 * lanes, 2 * lanes), 2 * lanes)],
+                part_sem.at[k // (GROUPS // 2)],
+            ).start()
+        return carry
 
     for copy in smalls:
         copy.start()
@@ -104,6 +107,9 @@
         return carry
 
     lax.fori_loop(1, n_ori, greet_ori, 0)
+
+    lax.fori_loop(0, CHUNKS * GROUPS // 2, fetch, 0)
+    smalls[0].wait()
 
     def exchange(first, second):
         for odd in range(2):
@@ -128,48 +134,40 @@
 
     pl.semaphore_wait(barrier, len(peers) + n_ori - 1)
 
-    def gather0(c, carry):
-        odd, v, u = axes(c)
-        at = v * 8 + u * 2 + my_z
-        send(mine.at[c], gath.at[c, at], ag_send.at[c], ag_recv.at[c, 0], device(odd, v, u, 1 - my_z))
+    def gather0(c):
+        odd, v, u = axes(c)
+        home = u * 2 + my_z
+        at = v * 8 + home
+
+        def share(i, carry):
+            q = (home + i) % 8
+            send(mine.at[c], gath.at[c, at], ag_send.at[c], ag_recv.at[c], device(odd, v, q // 2, q % 2))
+            return carry
+
+        lax.fori_loop(1, 8, share, 0)
         gath[c, at] = mine[c]
-        return carry
 
     def gather1(c):
         odd, v, u = axes(c)
-        wait(mine.at[c], ag_recv.at[c, 0])
-        pair = gath.at[c, pl.ds(v * 8 + u * 2, 2)]
-        send(pair, pair, ag_send.at[c], ag_recv.at[c, 1], device(odd, v, step(u, 1), my_z))
-        send(pair, pair, ag_send.at[c], ag_recv.at[c, 2], device(odd, v, step(u, 3), my_z))
+        wait(gath.at[c, pl.ds(0, 7)], ag_recv.at[c])
+        for first in range(2):
+            for k, by in ((0, 1), (1, 3)):
+                h = k if first == 0 else 1 - k
+                block = gath.at[c, pl.ds(v * 8 + h * half, half)]
+                send(block, block, ag_send.at[c], ag_near.at[c, k, h], device(odd, step(v, by), u, my_z))
 
     def gather2(c):
         odd, v, u = axes(c)
         for k, by in ((0, 1), (1, 3)):
-            came = v * 8 + step(u, 4 - by) * 2
-            wait(gath.at[c, pl.ds(came, 2)], ag_recv.at[c, 1 + k])
-            one = gath.at[c, came + k]
-            send(one, one, ag_send.at[c], ag_recv.at[c, 3 + k], device(odd, v, step(u, by), my_z))
+            block = gath.at[c, pl.ds(step(v, 4 - by) * 8 + k * half, half)]
+            wait(block, ag_near.at[c, k, k])
+            send(block, block, ag_send.at[c], ag_far.at[c, k], device(odd, step(v, by), u, my_z))
 
     def gather3(c):
-        odd, v, u = axes(c)
+        block = gath.at[c, pl.ds(0, half)]
         for k in range(2):
-            wait(gath.at[c, v * 8 + step(u, 2) * 2 + k], ag_recv.at[c, 3 + k])
-        block = gath.at[c, pl.ds(v * 8, 8)]
-        send(block, block, ag_send.at[c], ag_recv.at[c, 5], device(odd, step(v, 1), u, my_z))
-        send(block, block, ag_send.at[c], ag_recv.at[c, 6], device(odd, step(v, 3), u, my_z))
-
-    def gather4(c):
-        odd, v, u = axes(c)
-        for k, by in ((0, 1), (1, 3)):
-            came = step(v, 4 - by) * 8
-            wait(gath.at[c, pl.ds(came, 8)], ag_recv.at[c, 5 + k])
-            part_of = gath.at[c, pl.ds(came + k * half, half)]
-            send(part_of, part_of, ag_send.at[c], ag_recv.at[c, 7 + k], device(odd, step(v, by), u, my_z))
-
-    def gather5(c):
-        odd, v, u = axes(c)
-        for k in range(2):
-            wait(gath.at[c, pl.ds(step(v, 2) * 8 + k * half, half)], ag_recv.at[c, 7 + k])
+            wait(block, ag_near.at[c, k, 1 - k])
+            wait(block, ag_far.at[c, k])
 
     def pair(k, stage):
         def one(i, carry):
@@ -178,16 +176,10 @@
 
         lax.fori_loop(0, 2, one, 0)
 
-    lax.fori_loop(0, CHUNKS, gather0, 0)
-
-    def fetch(k, carry):
-        for copy in part_copies(k):
-            copy.start()
-        return carry
-
-    lax.fori_loop(0, CHUNKS * GROUPS, fetch, 0)
-    pair(0, gather1)
+    pair(0, gather0)
+    pair(1, gather0)
     exchange(perm, perm_t)
+    smalls[1].wait()
 
     shift_ids = lax.broadcasted_iota(jnp.int32, (shifts, 128), 0)
     off_x = jnp.zeros((shifts, 128), jnp.int32)
@@ -209,22 +201,22 @@
         return carry
 
     lax.fori_loop(0, freqs // 1024, tables, 0)
-    pair(0, gather2)
+    pair(0, gather1)
+    pair(2, gather0)
+    pair(3, gather0)
     pair(1, gather1)
     lax.fori_loop(freqs // 1024, freqs // 512, tables, 0)
-    pair(0, gather3)
-    pair(1, gather2)
-    for copy in smalls:
+    for copy in smalls[2:]:
         copy.wait()
     acc[...] = jnp.zeros_like(acc)
     power[...] = jnp.zeros_like(power)
-    pair(0, gather4)
-    pair(1, gather3)
+    pair(0, gather2)
+    pair(2, gather1)
 
     def score_chunk(c, carry):
         odd, v, u = axes(c)
         wait(part.at[:, pl.ds(0, 2 * width)], part_sem.at[c])
-        gather5(c)
+        gather3(c)
 
         for h in range(2):
             spread = jnp.dot(
@@ -235,12 +227,11 @@
                     rows[q, pl.ds(tile_row(odd, h, k), 8), :] = spread[q * 32 + k * 8:q * 32 + k * 8 + 8, :]
 
         for g in range(GROUPS):
-            base = pl.multiple_of(c * width + g * lanes, lanes)
             for j in range(lanes // 128):
-                at = pl.ds(j * 128, 128)
-                there = pl.ds(pl.multiple_of(base + j * 128, 128), 128)
-                real = rows[g, :, at]
-                imag = rows[GROUPS + g, :, at]
+                col = g % 2 * lanes + j * 128
+                there = pl.ds(pl.multiple_of(c * width + g * lanes + j * 128, 128), 128)
+                real = rows[g, :, pl.ds(j * 128, 128)]
+                imag = rows[GROUPS + g, :, pl.ds(j * 128, 128)]
                 inv = inv_ref[:, there]
                 re = real * inv
                 im = imag * inv
@@ -248,18 +239,23 @@
                 for t in range(shifts):
                     cosine = cos_tab[pl.ds(t, 1), there]
                     sine = sin_tab[pl.ds(t, 1), there]
-                    into = lhs.at[g % 2, pl.ds(t * slots, slots)]
-                    into[:, at] = (re * cosine + im * sine).astype(BF16)
-                    into[:, pl.ds(lanes + j * 128, 128)] = (im * cosine - re * sine).astype(BF16)
-            acc[...] += lax.dot_general(
-                lhs[g % 2], part[:, pl.ds(pl.multiple_of(2 * base, 2 * lanes), 2 * lanes)],
-                (((1,), (1,)), ((), ())), preferred_element_type=F32,
-            )
-
-        for k in range(CHUNKS // 2):
-            @pl.when(c == k)
-            def _():
-                gather4(CHUNKS // 2 + k)
+                    into = lhs.at[g // 2 % 2, pl.ds(t * slots, slots)]
+                    into[:, pl.ds(col, 128)] = (re * cosine + im * sine).astype(BF16)
+                    into[:, pl.ds(2 * lanes + col, 128)] = (im * cosine - re * sine).astype(BF16)
+            if g % 2 == 1:
+                base = pl.multiple_of(2 * (c * width + (g - 1) * lanes), 4 * lanes)
+                acc[...] += lax.dot_general(
+                    lhs[g // 2 % 2], part[:, pl.ds(base, 4 * lanes)],
+                    (((1,), (1,)), ((), ())), preferred_element_type=F32,
+                )
+
+        @pl.when((c % 2 == 0) & (c < CHUNKS - 2))
+        def _():
+            pair(c // 2 + 1, gather2)
+
+        @pl.when((c % 2 == 1) & (c < CHUNKS - 6))
+        def _():
+            pair(c // 2 + 3, gather1)
 
         return carry
 
@@ -309,22 +305,24 @@
         odd, v, u = axes(c)
 
         def multiply(g):
-            base = pl.multiple_of(2 * (c * width + g * lanes), 2 * lanes)
-            prods[g % 2] = jnp.dot(by_class[...], part[:, pl.ds(base, 2 * lanes)], preferred_element_type=F32)
+            base = pl.multiple_of(2 * (c * width + 2 * g * lanes), 4 * lanes)
+            prods[g % 2] = jnp.dot(by_class[...], part[:, pl.ds(base, 4 * lanes)], preferred_element_type=F32)
 
         multiply(0)
         for g in range(GROUPS):
-            if g + 1 < GROUPS:
-                multiply(g + 1)
+            if g % 2 == 0 and g // 2 + 1 < GROUPS // 2:
+                multiply(g // 2 + 1)
             for j in range(lanes // 128):
                 at = pl.ds(j * 128, 128)
+                col = g % 2 * lanes + j * 128
                 there = pl.ds(pl.multiple_of(c * width + g * lanes + j * 128, 128), 128)
                 out_real = out_imag = None
                 for t in range(shifts):
                     cosine = cos_tab[pl.ds(t, 1), there]
                     sine = sin_tab[pl.ds(t, 1), there]
-                    re = prods[g % 2, pl.ds(t * slots, slots), at]
-                    im = prods[g % 2, pl.ds(t * slots, slots), pl.ds(lanes + j * 128, 128)]
+                    block = prods.at[g // 2 % 2, pl.ds(t * slots, slots)]
+                    re = block[:, pl.ds(col, 128)]
+                    im = block[:, pl.ds(2 * lanes + col, 128)]
                     term_real = re * cosine - im * sine
                     term_imag = im * cosine + re * sine
                     out_real = term_real if t == 0 else out_real + term_real
@@ -397,17 +395,17 @@
             sum_chunk(i)
             reduce0(i)
 
-        @pl.when((i >= 1) & (i < CHUNKS + 1))
+        @pl.when((i >= LAG) & (i < CHUNKS + LAG))
         def _():
-            reduce1(i - 1)
-
-        @pl.when(i >= 2)
+            reduce1(i - LAG)
+
+        @pl.when(i >= 2 * LAG)
         def _():
-            reduce2(i - 2)
-
-        return carry
-
-    lax.fori_loop(0, CHUNKS + 2, sum_step, 0)
+            reduce2(i - 2 * LAG)
+
+        return carry
+
+    lax.fori_loop(0, CHUNKS + 2 * LAG, sum_step, 0)
 
     for c in range(CHUNKS):
         wait(recv2.at[c, pl.ds(0, 7)], rs_recv.at[c])
@@ -437,7 +435,7 @@
     slots = 2 * n_dom
     lanes = freqs // (CHUNKS * GROUPS)
     vmem = pl.BlockSpec(memory_space=pltpu.VMEM)
-    anywhere = pl.BlockSpec(memory_space=pl.ANY)
+    far = pl.BlockSpec(memory_space=pltpu.HBM)
     dma = pltpu.SemaphoreType.DMA
     sums, loglik = pl.pallas_call(
         functools.partial(em_kernel, n_dom, n_ori, shifts),
@@ -445,7 +443,7 @@
             jax.ShapeDtypeStruct((2, 1, feat), F32),
             jax.ShapeDtypeStruct((1, pcount), F32),
         ),
-        in_specs=[vmem, anywhere, anywhere, pl.BlockSpec(memory_space=pltpu.SMEM), anywhere, anywhere],
+        in_specs=[far] * 6,
         out_specs=(vmem, vmem),
         scratch_shapes=[
             pltpu.VMEM((pcount, feat), BF16),
@@ -457,10 +455,12 @@
             pltpu.VMEM((2, 256, 256), BF16),
             pltpu.VMEM((shifts, freqs), F32),
             pltpu.VMEM((shifts, freqs), F32),
-            pltpu.VMEM((2, shifts * slots, 2 * lanes), BF16),
+            pltpu.VMEM((2, shifts * slots, 4 * lanes), BF16),
             pltpu.VMEM((shifts * slots, pcount), F32),
-            pltpu.VMEM((2, shifts * slots, 2 * lanes), F32),
+            pltpu.VMEM((2, shifts * slots, 4 * lanes), F32),
             pltpu.VMEM((slots, 128), F32),
+            pltpu.VMEM((2, feat), BF16),
+            pltpu.SMEM((2, shifts), jnp.int32),
             pltpu.VMEM((1, freqs), F32),
             pltpu.VMEM((1, slots), jnp.int32),
             pltpu.VMEM((1, pcount), jnp.int32),
@@ -473,9 +473,11 @@
             pltpu.VMEM((CHUNKS, 8, 16, lanes), BF16),
             pltpu.VMEM((CHUNKS, 8, 16, lanes), BF16),
             dma((CHUNKS,)),
-            dma((3,)),
+            dma((5,)),
             dma((CHUNKS,)),
-            dma((CHUNKS, 9)),
+            dma((CHUNKS,)),
+            dma((CHUNKS, 2, 2)),
+            dma((CHUNKS, 2)),
             dma,
             dma,
             dma((CHUNKS,)),

time: 77.9 us -> 75.1 us (0.964); the launches traced: 76.9 us -> 75 us
  Pallas kernels: 73.5 us -> 71.5 us
    pallas_call x1, Pallas kernels: 73.5 us -> 71.5 us  [per_device(): pl.pallas_call(functools.partial(em_kernel, n_dom, n_ori, shifts), out_sh...]
where the time goes in v2:
time: 75.1 us; the launch traced here: 75 us
  Pallas kernels  71.5 us (95%)
  local copies, waits for them, and re-layouts  2.8 us (4%)
    pallas_call x1, Pallas kernels, per_device(): pl.pallas_call(functools.partial(em_kernel, n_dom, n_ori, shifts), out_sh...  71.5 us
    unnamed x2, local copies, waits for them, and re-layouts  2.8 us

profile of v2, /device:TPU:2, one launch (start us, length us, event | category | flops | bytes accessed | tf_op | source)
XLA Modules:
  0.0 75.0 jit_solution(9832494407959937503)
XLA Ops:
  0.6 71.5 %shard_map.77 = (f32[2,1,16384]{2,1,0:T(1,128)}, f32[1,256]{1,0:T(1,128)}) custom-call(bf16[2,16384]{1,0:T(2,128)(2,1)} %bitcast.7, bf16[256,16384]{1,0:T(8,128)(2,1)} %part_hbm.1, f32[1,8192]{1,0:T(1,128)} %bitcast.8, s32[2,9]{1,0:T(2,128)} %bitcast.9, s32[1,64]{1,0:T(1,128)} %bitcast.11, s32[1,256]{1,0:T(1,128)} %bitcast.10), custom_call_target="tpu_custom_call" | custom-call | flops 9663676416 | bytes 8388608 | tf_op jit(solution)/shard_map/pallas_call | solution.py:440
  72.2 1.6 %copy.10 = f32[2,1,16384]{2,1,0:T(1,128)} copy(f32[2,1,16384]{2,1,0:T(1,128)} %get-tuple-element.8) | data formatting | bytes 262144
  73.8 1.2 %copy.11 = f32[256]{0:T(256)} copy(f32[256]{0:T(256)} %bitcast.6) | data formatting | bytes 2048

commit v3 on v2

--- a/solution.py
+++ b/solution.py
@@ -36,7 +36,7 @@
     n_dom, n_ori, shifts,
     refs_hbm, part_hbm, inv_hbm, off_hbm, omap_hbm, center_hbm,
     out_ref, loglik_ref,
-    part, stage, mine, gath, rows, perm, perm_t, cos_tab, sin_tab, lhs, acc, prods, power, refs_ref, off_ref, inv_ref, omap_ref, center_ref,
+    part, part_t, stage, mine, gath, rows, perm, perm_t, cos_tab, sin_tab, lhs, acc, prods, power, refs_ref, off_ref, inv_ref, omap_ref, center_ref,
     stat_out, stat_in, by_class, sends, far_in, near_in, send2, recv2,
     part_sem, small_sem, ag_send, ag_recv, ag_near, ag_far, st_send, st_recv, rs_send, far_sem, early_sem, late_sem, rs_recv,
 ):
@@ -176,6 +176,16 @@
 
         lax.fori_loop(0, 2, one, 0)
 
+    def turn(k, carry):
+        at = pl.ds(pl.multiple_of(k * 4 * lanes, 4 * lanes), 4 * lanes)
+        part_t[at, :] = part[:, at].T
+        return carry
+
+    def turn_pair(k):
+        for c in (2 * k, 2 * k + 1):
+            wait(part.at[:, pl.ds(0, 2 * width)], part_sem.at[c])
+        lax.fori_loop(2 * k * GROUPS // 2, (2 * k + 2) * GROUPS // 2, turn, 0)
+
     pair(0, gather0)
     pair(1, gather0)
     exchange(perm, perm_t)
@@ -201,21 +211,24 @@
         return carry
 
     lax.fori_loop(0, freqs // 1024, tables, 0)
+    turn_pair(0)
     pair(0, gather1)
     pair(2, gather0)
     pair(3, gather0)
     pair(1, gather1)
     lax.fori_loop(freqs // 1024, freqs // 512, tables, 0)
+    turn_pair(1)
     for copy in smalls[2:]:
         copy.wait()
     acc[...] = jnp.zeros_like(acc)
     power[...] = jnp.zeros_like(power)
     pair(0, gather2)
+    turn_pair(2)
     pair(2, gather1)
+    turn_pair(3)
 
     def score_chunk(c, carry):
         odd, v, u = axes(c)
-        wait(part.at[:, pl.ds(0, 2 * width)], part_sem.at[c])
         gather3(c)
 
         for h in range(2):
@@ -244,10 +257,7 @@
                     into[:, pl.ds(2 * lanes + col, 128)] = (im * cosine - re * sine).astype(BF16)
             if g % 2 == 1:
                 base = pl.multiple_of(2 * (c * width + (g - 1) * lanes), 4 * lanes)
-                acc[...] += lax.dot_general(
-                    lhs[g // 2 % 2], part[:, pl.ds(base, 4 * lanes)],
-                    (((1,), (1,)), ((), ())), preferred_element_type=F32,
-                )
+                acc[...] += jnp.dot(lhs[g // 2 % 2], part_t[pl.ds(base, 4 * lanes), :], preferred_element_type=F32)
 
         @pl.when((c % 2 == 0) & (c < CHUNKS - 2))
         def _():
@@ -447,6 +457,7 @@
         out_specs=(vmem, vmem),
         scratch_shapes=[
             pltpu.VMEM((pcount, feat), BF16),
+            pltpu.VMEM((feat, pcount), BF16),
             pltpu.VMEM((lanes // 128, 16 * CHUNKS, 128), F32),
             pltpu.VMEM((CHUNKS, 16, lanes), BF16),
             pltpu.VMEM((CHUNKS, n_dom, 16, lanes), BF16),

time: 75.1 us -> 74.4 us (level)
  no operation moved by 1% of the time
where the time goes in v3:
time: 74.4 us; the launch traced here: 74.3 us
  Pallas kernels  70.9 us (95%)
  local copies, waits for them, and re-layouts  2.8 us (4%)
    pallas_call x1, Pallas kernels, per_device(): pl.pallas_call(functools.partial(em_kernel, n_dom, n_ori, shifts), out_sh...  70.9 us
    unnamed x2, local copies, waits for them, and re-layouts  2.8 us

profile of v3, /device:TPU:2, one launch (start us, length us, event | category | flops | bytes accessed | tf_op | source)
XLA Modules:
  0.0 74.3 jit_solution(7684887261293549301)
XLA Ops:
  0.6 70.9 %shard_map.77 = (f32[2,1,16384]{2,1,0:T(1,128)}, f32[1,256]{1,0:T(1,128)}) custom-call(bf16[2,16384]{1,0:T(2,128)(2,1)} %bitcast.7, bf16[256,16384]{1,0:T(8,128)(2,1)} %part_hbm.1, f32[1,8192]{1,0:T(1,128)} %bitcast.8, s32[2,9]{1,0:T(2,128)} %bitcast.9, s32[1,64]{1,0:T(1,128)} %bitcast.11, s32[1,256]{1,0:T(1,128)} %bitcast.10), custom_call_target="tpu_custom_call" | custom-call | flops 9663676416 | bytes 8388608 | tf_op jit(solution)/shard_map/pallas_call | solution.py:450
  71.5 1.6 %copy.10 = f32[2,1,16384]{2,1,0:T(1,128)} copy(f32[2,1,16384]{2,1,0:T(1,128)} %get-tuple-element.8) | data formatting | bytes 262144
  73.1 1.2 %copy.11 = f32[256]{0:T(256)} copy(f32[256]{0:T(256)} %bitcast.6) | data formatting | bytes 2048

commit v4 on v3

--- a/solution.py
+++ b/solution.py
@@ -32,43 +32,88 @@
     return jnp.where(odd, sine, cosine) * cos_sign, jnp.where(odd, cosine, sine) * sin_sign
 
 
+class Torus:
+    def __init__(self):
+        self.me = lax.axis_index("dom")
+        self.y, self.x, self.z = self.me // 8, (self.me // 2) % 4, self.me % 2
+
+    def axes(self, c, odd=None):
+        odd = c % 2 if odd is None else odd
+        return odd, self.y * (1 - odd) + self.x * odd, self.x * (1 - odd) + self.y * odd
+
+    def peers(self):
+        near = [device(0, self.y, self.x, 1 - self.z)]
+        for by in (1, 2, 3):
+            for z in (self.z, 1 - self.z):
+                near.append(device(0, self.y, step(self.x, by), z))
+                near.append(device(0, step(self.y, by), self.x, z))
+        return near
+
+
+def device(odd, v, u, z):
+    return {"dom": ((v * (1 - odd) + u * odd) * 4 + u * (1 - odd) + v * odd) * 2 + z}
+
+
+def step(a, by):
+    return (a + by) % RING
+
+
+def tile_row(odd, h, k):
+    return pl.multiple_of((32 * h + 8 * k) * (1 - odd) + (16 * k + 8 * h) * odd, 8)
+
+
+def greet(barrier, to):
+    pl.semaphore_signal(barrier, inc=1, device_id=to, device_id_type=MESH)
+
+
+def send(src, dst, send_sem, recv_sem, to):
+    pltpu.make_async_remote_copy(
+        src_ref=src, dst_ref=dst, send_sem=send_sem, recv_sem=recv_sem, device_id=to, device_id_type=MESH
+    ).start()
+
+
+def wait(ref, sem):
+    pltpu.make_async_copy(ref, ref, sem).wait()
+
+
+def fetch_particles(part_hbm, part, part_sem, freqs):
+    width = freqs // CHUNKS
+    for c in range(CHUNKS):
+        for base in (0, freqs):
+            cols = pl.ds(base + c * width, width)
+            pltpu.make_async_copy(part_hbm.at[:, cols], part.at[:, cols], part_sem.at[c]).start()
+
+
+def exchange(perm, perm_t):
+    for odd, ref, inverse in ((0, perm, 0), (1, perm, 0), (0, perm_t, 1), (1, perm_t, 1)):
+        there = lax.broadcasted_iota(jnp.int32, (256, 256), 0)
+        here = lax.broadcasted_iota(jnp.int32, (256, 256), 1)
+        out, src = (here, there) if inverse else (there, here)
+        at, s, q = src >> 4, (src >> 3) & 1, src & 7
+        if odd:
+            row = ((at >> 1) & 3) * 8 + (at >> 3) * 4 + (at & 1) * 2 + s
+        else:
+            row = at * 2 + s
+        ref[odd] = (out == q * 32 + row).astype(F32).astype(BF16)
+
+
 def em_kernel(
     n_dom, n_ori, shifts,
     refs_hbm, part_hbm, inv_hbm, off_hbm, omap_hbm, center_hbm,
-    out_ref, loglik_ref,
-    part, part_t, stage, mine, gath, rows, perm, perm_t, cos_tab, sin_tab, lhs, acc, prods, power, refs_ref, off_ref, inv_ref, omap_ref, center_ref,
-    stat_out, stat_in, by_class, sends, far_in, near_in, send2, recv2,
-    part_sem, small_sem, ag_send, ag_recv, ag_near, ag_far, st_send, st_recv, rs_send, far_sem, early_sem, late_sem, rs_recv,
+    recv2, loglik_ref,
+    part, part_t, stage, mine, gath, rows, perm, perm_t, cos_tab, sin_tab, lhs_a, lhs_b, acc, prods_a, prods_b, power,
+    refs_ref, off_ref, inv_ref, omap_ref, center_ref, stat_out, stat_in, by_class, sends, far_in, near_in, send2,
+    part_sem, small_sem, ag_send, ag_recv, ag_near, ag_far, st_send, st_recv,
+    rs_send, far_sem, early_sem, late_sem, rs_recv,
 ):
     freqs = inv_ref.shape[1]
     slots = 2 * n_dom
     lanes = mine.shape[2]
     width = freqs // CHUNKS
     half = RING
-    me = lax.axis_index("dom")
+    here = Torus()
+    axes, my_z = here.axes, here.z
     my_ori = lax.axis_index("orient")
-    my_y, my_x, my_z = me // 8, (me // 2) % 4, me % 2
-
-    def axes(c):
-        odd = c % 2
-        return odd, my_y * (1 - odd) + my_x * odd, my_x * (1 - odd) + my_y * odd
-
-    def device(odd, v, u, z):
-        return {"dom": ((v * (1 - odd) + u * odd) * 4 + u * (1 - odd) + v * odd) * 2 + z}
-
-    def step(a, by):
-        return (a + by) % RING
-
-    def tile_row(odd, h, k):
-        return pl.multiple_of((32 * h + 8 * k) * (1 - odd) + (16 * k + 8 * h) * odd, 8)
-
-    def send(src, dst, send_sem, recv_sem, to):
-        pltpu.make_async_remote_copy(
-            src_ref=src, dst_ref=dst, send_sem=send_sem, recv_sem=recv_sem, device_id=to, device_id_type=MESH
-        ).start()
-
-    def wait(ref, sem):
-        pltpu.make_async_copy(ref, ref, sem).wait()
 
     smalls = [
         pltpu.make_async_copy(src, dst, small_sem.at[k])
@@ -77,51 +122,21 @@
         ))
     ]
 
-    def fetch(k, carry):
-        for r, base in enumerate((0, freqs)):
-            pltpu.make_async_copy(
-                part_hbm.at[:, pl.ds(pl.multiple_of(base + k * 2 * lanes, 2 * lanes), 2 * lanes)],
-                part.at[:, pl.ds(pl.multiple_of((2 * k + r) * 2 * lanes, 2 * lanes), 2 * lanes)],
-                part_sem.at[k // (GROUPS // 2)],
-            ).start()
-        return carry
-
     for copy in smalls:
         copy.start()
 
     barrier = pltpu.get_barrier_semaphore()
-
-    def greet(to):
-        pl.semaphore_signal(barrier, inc=1, device_id=to, device_id_type=MESH)
-
-    peers = [device(0, my_y, my_x, 1 - my_z)]
-    for by in (1, 2, 3):
-        for z in (my_z, 1 - my_z):
-            peers.append(device(0, my_y, step(my_x, by), z))
-            peers.append(device(0, step(my_y, by), my_x, z))
+    peers = here.peers()
     for to in peers:
-        greet(to)
+        greet(barrier, to)
 
     def greet_ori(i, carry):
-        greet({"orient": lax.rem(my_ori + i, n_ori)})
+        greet(barrier, {"orient": lax.rem(my_ori + i, n_ori)})
         return carry
 
     lax.fori_loop(1, n_ori, greet_ori, 0)
-
-    lax.fori_loop(0, CHUNKS * GROUPS // 2, fetch, 0)
+    fetch_particles(part_hbm, part, part_sem, freqs)
     smalls[0].wait()
-
-    def exchange(first, second):
-        for odd in range(2):
-            there = lax.broadcasted_iota(jnp.int32, (256, 256), 0)
-            here = lax.broadcasted_iota(jnp.int32, (256, 256), 1)
-            for ref, out, src in ((first, there, here), (second, here, there)):
-                at, s, q = src >> 4, (src >> 3) & 1, src & 7
-                if odd:
-                    row = ((at >> 1) & 3) * 8 + (at >> 3) * 4 + (at & 1) * 2 + s
-                else:
-                    row = at * 2 + s
-                ref[odd] = (out == q * 32 + row).astype(F32).astype(BF16)
 
     for c in range(CHUNKS):
         for r in range(2):
@@ -176,15 +191,16 @@
 
         lax.fori_loop(0, 2, one, 0)
 
-    def turn(k, carry):
-        at = pl.ds(pl.multiple_of(k * 4 * lanes, 4 * lanes), 4 * lanes)
-        part_t[at, :] = part[:, at].T
-        return carry
-
     def turn_pair(k):
         for c in (2 * k, 2 * k + 1):
             wait(part.at[:, pl.ds(0, 2 * width)], part_sem.at[c])
-        lax.fori_loop(2 * k * GROUPS // 2, (2 * k + 2) * GROUPS // 2, turn, 0)
+
+        def turn(i, carry):
+            at = pl.ds(pl.multiple_of(i // 4 * freqs + k * 2 * width + i % 4 * (width // 2), width // 2), width // 2)
+            part_t[at, :] = part[:, at].T
+            return carry
+
+        lax.fori_loop(0, 8, turn, 0)
 
     pair(0, gather0)
     pair(1, gather0)
@@ -211,26 +227,48 @@
         return carry
 
     lax.fori_loop(0, freqs // 1024, tables, 0)
-    turn_pair(0)
     pair(0, gather1)
     pair(2, gather0)
+    lax.fori_loop(freqs // 1024, freqs // 512, tables, 0)
+    pair(1, gather1)
+    turn_pair(0)
+    pair(0, gather2)
     pair(3, gather0)
-    pair(1, gather1)
-    lax.fori_loop(freqs // 1024, freqs // 512, tables, 0)
     turn_pair(1)
+    pair(2, gather1)
     for copy in smalls[2:]:
         copy.wait()
     acc[...] = jnp.zeros_like(acc)
     power[...] = jnp.zeros_like(power)
-    pair(0, gather2)
-    turn_pair(2)
-    pair(2, gather1)
-    turn_pair(3)
+    lhs_b[...] = jnp.zeros_like(lhs_b)
+
+    def columns(group):
+        at = pl.multiple_of(group * lanes, lanes)
+        return pl.ds(at, lanes), pl.ds(pl.multiple_of(freqs + at, lanes), lanes)
+
+    def score_product(lhs, group):
+        block = jnp.concatenate([part_t[at, :] for at in columns(group)], axis=0)
+        acc[...] += jnp.dot(lhs[...], block, preferred_element_type=F32)
+
+    def shift(lhs, c, g):
+        for j in range(lanes // 128):
+            there = pl.ds(pl.multiple_of((c * GROUPS + g) * lanes + j * 128, 128), 128)
+            real = rows[g, :, pl.ds(j * 128, 128)]
+            imag = rows[GROUPS + g, :, pl.ds(j * 128, 128)]
+            inv = inv_ref[:, there]
+            re = real * inv
+            im = imag * inv
+            power[...] += re * real + im * imag
+            for t in range(shifts):
+                cosine = cos_tab[pl.ds(t, 1), there]
+                sine = sin_tab[pl.ds(t, 1), there]
+                into = lhs.at[pl.ds(t * slots, slots)]
+                into[:, pl.ds(j * 128, 128)] = (re * cosine + im * sine).astype(BF16)
+                into[:, pl.ds(lanes + j * 128, 128)] = (im * cosine - re * sine).astype(BF16)
 
     def score_chunk(c, carry):
-        odd, v, u = axes(c)
+        odd = c % 2
         gather3(c)
-
         for h in range(2):
             spread = jnp.dot(
                 perm[odd], gath[c, pl.ds(16 * h, 16)].reshape(256, lanes), preferred_element_type=F32
@@ -239,37 +277,34 @@
                 for k in range(4):
                     rows[q, pl.ds(tile_row(odd, h, k), 8), :] = spread[q * 32 + k * 8:q * 32 + k * 8 + 8, :]
 
-        for g in range(GROUPS):
-            for j in range(lanes // 128):
-                col = g % 2 * lanes + j * 128
-                there = pl.ds(pl.multiple_of(c * width + g * lanes + j * 128, 128), 128)
-                real = rows[g, :, pl.ds(j * 128, 128)]
-                imag = rows[GROUPS + g, :, pl.ds(j * 128, 128)]
-                inv = inv_ref[:, there]
-                re = real * inv
-                im = imag * inv
-                power[...] += re * real + im * imag
-                for t in range(shifts):
-                    cosine = cos_tab[pl.ds(t, 1), there]
-                    sine = sin_tab[pl.ds(t, 1), there]
-                    into = lhs.at[g // 2 % 2, pl.ds(t * slots, slots)]
-                    into[:, pl.ds(col, 128)] = (re * cosine + im * sine).astype(BF16)
-                    into[:, pl.ds(2 * lanes + col, 128)] = (im * cosine - re * sine).astype(BF16)
-            if g % 2 == 1:
-                base = pl.multiple_of(2 * (c * width + (g - 1) * lanes), 4 * lanes)
-                acc[...] += jnp.dot(lhs[g // 2 % 2], part_t[pl.ds(base, 4 * lanes), :], preferred_element_type=F32)
-
-        @pl.when((c % 2 == 0) & (c < CHUNKS - 2))
+        def two_groups(i, carry):
+            first = c * GROUPS + 2 * i
+            score_product(lhs_b, jnp.maximum(first - 1, 0))
+            shift(lhs_a, c, 2 * i)
+            score_product(lhs_a, first)
+            shift(lhs_b, c, 2 * i + 1)
+            return carry
+
+        lax.fori_loop(0, GROUPS // 2, two_groups, 0)
+
+        for k in range(PAIRS - 1):
+            @pl.when(c == 2 * k)
+            def _():
+                pair(k + 1, gather2)
+
+        @pl.when(c == 1)
         def _():
-            pair(c // 2 + 1, gather2)
-
-        @pl.when((c % 2 == 1) & (c < CHUNKS - 6))
-        def _():
-            pair(c // 2 + 3, gather1)
+            pair(PAIRS - 1, gather1)
+
+        for k in range(2, PAIRS):
+            @pl.when(c == 2 * k - 3)
+            def _():
+                turn_pair(k)
 
         return carry
 
     lax.fori_loop(0, CHUNKS, score_chunk, 0)
+    score_product(lhs_b, CHUNKS * GROUPS - 1)
 
     power_col = 0.5 * jnp.sum(power[...], axis=1, keepdims=True)
     distance = jnp.abs(my_ori - center_ref[...])
@@ -311,35 +346,39 @@
     for t in range(shifts):
         by_class[pl.ds(t * slots, slots), :] = picked[:, t * pcount:(t + 1) * pcount]
 
+    def multiply(prods, group):
+        block = jnp.concatenate([part[:, at] for at in columns(group)], axis=1)
+        prods[...] = jnp.dot(by_class[...], block, preferred_element_type=F32)
+
+    def rotate(prods, c, g):
+        for j in range(lanes // 128):
+            at = pl.ds(j * 128, 128)
+            there = pl.ds(pl.multiple_of((c * GROUPS + g) * lanes + j * 128, 128), 128)
+            out_real = out_imag = None
+            for t in range(shifts):
+                cosine = cos_tab[pl.ds(t, 1), there]
+                sine = sin_tab[pl.ds(t, 1), there]
+                re = prods[pl.ds(t * slots, slots), at]
+                im = prods[pl.ds(t * slots, slots), pl.ds(lanes + j * 128, 128)]
+                term_real = re * cosine - im * sine
+                term_imag = im * cosine + re * sine
+                out_real = term_real if t == 0 else out_real + term_real
+                out_imag = term_imag if t == 0 else out_imag + term_imag
+            rows[g, :, at] = out_real
+            rows[GROUPS + g, :, at] = out_imag
+
     def sum_chunk(c):
-        odd, v, u = axes(c)
-
-        def multiply(g):
-            base = pl.multiple_of(2 * (c * width + 2 * g * lanes), 4 * lanes)
-            prods[g % 2] = jnp.dot(by_class[...], part[:, pl.ds(base, 4 * lanes)], preferred_element_type=F32)
-
-        multiply(0)
-        for g in range(GROUPS):
-            if g % 2 == 0 and g // 2 + 1 < GROUPS // 2:
-                multiply(g // 2 + 1)
-            for j in range(lanes // 128):
-                at = pl.ds(j * 128, 128)
-                col = g % 2 * lanes + j * 128
-                there = pl.ds(pl.multiple_of(c * width + g * lanes + j * 128, 128), 128)
-                out_real = out_imag = None
-                for t in range(shifts):
-                    cosine = cos_tab[pl.ds(t, 1), there]
-                    sine = sin_tab[pl.ds(t, 1), there]
-                    block = prods.at[g // 2 % 2, pl.ds(t * slots, slots)]
-                    re = block[:, pl.ds(col, 128)]
-                    im = block[:, pl.ds(2 * lanes + col, 128)]
-                    term_real = re * cosine - im * sine
-                    term_imag = im * cosine + re * sine
-                    out_real = term_real if t == 0 else out_real + term_real
-                    out_imag = term_imag if t == 0 else out_imag + term_imag
-                rows[g, :, at] = out_real
-                rows[GROUPS + g, :, at] = out_imag
-
+        odd = c % 2
+
+        def two_groups(i, carry):
+            first = c * GROUPS + 2 * i
+            multiply(prods_b, first + 1)
+            rotate(prods_a, c, 2 * i)
+            multiply(prods_a, jnp.minimum(first + 2, CHUNKS * GROUPS - 1))
+            rotate(prods_b, c, 2 * i + 1)
+            return carry
+
+        lax.fori_loop(0, GROUPS // 2, two_groups, 0)
         for h in range(2):
             tiles = [rows[q, pl.ds(tile_row(odd, h, k), 8), :] for q in range(8) for k in range(4)]
             spread = jnp.dot(
@@ -399,26 +438,41 @@
         lax.fori_loop(1, 8, share, 0)
         recv2[c, home] = send2[c, home]
 
-    def sum_step(i, carry):
-        @pl.when(i < CHUNKS)
+    def progress(c):
+        @pl.when((c >= LAG) & (c < CHUNKS + LAG))
         def _():
-            sum_chunk(i)
-            reduce0(i)
-
-        @pl.when((i >= LAG) & (i < CHUNKS + LAG))
+            reduce1(c - LAG)
+
+        @pl.when(c >= 2 * LAG)
         def _():
-            reduce1(i - LAG)
-
-        @pl.when(i >= 2 * LAG)
+            reduce2(c - 2 * LAG)
+
+    def sum_step(c, carry):
+        @pl.when(c < CHUNKS)
         def _():
-            reduce2(i - 2 * LAG)
-
+            sum_chunk(c)
+            reduce0(c)
+
+        progress(c)
         return carry
 
+    multiply(prods_a, 0)
     lax.fori_loop(0, CHUNKS + 2 * LAG, sum_step, 0)
 
+    def drain(c, carry):
+        wait(recv2.at[c, pl.ds(0, 7)], rs_recv.at[c])
+        wait(gath.at[c, pl.ds(0, n_dom - 1)], ag_send.at[c])
+        wait(sends.at[c, pl.ds(0, 31)], rs_send.at[c])
+        return carry
+
+    lax.fori_loop(0, CHUNKS, drain, 0)
+
+
+def last_kernel(recv2, loglik_in, out_ref, loglik_ref):
+    lanes = recv2.shape[3]
+    freqs = CHUNKS * GROUPS * lanes
+    loglik_ref[...] = loglik_in[...]
     for c in range(CHUNKS):
-        wait(recv2.at[c, pl.ds(0, 7)], rs_recv.at[c])
         for j in range(lanes // 128):
             total = recv2[c, 0, :, pl.ds(j * 128, 128)].astype(F32)
             for q in range(1, 8):
@@ -427,15 +481,8 @@
                 for r in range(2):
                     for g in range(GROUPS):
                         row = s * 8 + r * GROUPS + g
-                        at = r * freqs + c * width + g * lanes + j * 128
+                        at = r * freqs + c * GROUPS * lanes + g * lanes + j * 128
                         out_ref[s, :, pl.ds(at, 128)] = total[row:row + 1, :]
-
-    def drain(c, carry):
-        wait(gath.at[c, pl.ds(0, n_dom - 1)], ag_send.at[c])
-        wait(gath.at[c, pl.ds(0, 31)], rs_send.at[c])
-        return carry
-
-    lax.fori_loop(0, CHUNKS, drain, 0)
 
 
 def per_device(n_dom, n_ori, particles, refs, inv_sigma2, offsets, owner_map, center):
@@ -447,10 +494,11 @@
     vmem = pl.BlockSpec(memory_space=pltpu.VMEM)
     far = pl.BlockSpec(memory_space=pltpu.HBM)
     dma = pltpu.SemaphoreType.DMA
-    sums, loglik = pl.pallas_call(
+    grant = 56 * 1024 * 1024
+    partial, loglik = pl.pallas_call(
         functools.partial(em_kernel, n_dom, n_ori, shifts),
         out_shape=(
-            jax.ShapeDtypeStruct((2, 1, feat), F32),
+            jax.ShapeDtypeStruct((CHUNKS, 8, 16, lanes), BF16),
             jax.ShapeDtypeStruct((1, pcount), F32),
         ),
         in_specs=[far] * 6,
@@ -466,9 +514,11 @@
             pltpu.VMEM((2, 256, 256), BF16),
             pltpu.VMEM((shifts, freqs), F32),
             pltpu.VMEM((shifts, freqs), F32),
-            pltpu.VMEM((2, shifts * slots, 4 * lanes), BF16),
+            pltpu.VMEM((shifts * slots, 2 * lanes), BF16),
+            pltpu.VMEM((shifts * slots, 2 * lanes), BF16),
             pltpu.VMEM((shifts * slots, pcount), F32),
-            pltpu.VMEM((2, shifts * slots, 4 * lanes), F32),
+            pltpu.VMEM((shifts * slots, 2 * lanes), F32),
+            pltpu.VMEM((shifts * slots, 2 * lanes), F32),
             pltpu.VMEM((slots, 128), F32),
             pltpu.VMEM((2, feat), BF16),
             pltpu.SMEM((2, shifts), jnp.int32),
@@ -481,7 +531,6 @@
             pltpu.VMEM((CHUNKS, n_dom, 16, lanes), BF16),
             pltpu.VMEM((CHUNKS, 2, RING, 16, lanes), BF16),
             pltpu.VMEM((CHUNKS, 2, 8, 16, lanes), BF16),
-            pltpu.VMEM((CHUNKS, 8, 16, lanes), BF16),
             pltpu.VMEM((CHUNKS, 8, 16, lanes), BF16),
             dma((CHUNKS,)),
             dma((5,)),
@@ -497,9 +546,7 @@
             dma((CHUNKS, 2)),
             dma((CHUNKS,)),
         ],
-        compiler_params=pltpu.CompilerParams(
-            collective_id=0, has_side_effects=True, vmem_limit_bytes=56 * 1024 * 1024
-        ),
+        compiler_params=pltpu.CompilerParams(collective_id=0, has_side_effects=True, vmem_limit_bytes=grant),
         cost_estimate=pl.CostEstimate(
             flops=4 * shifts * slots * pcount * feat, bytes_accessed=2 * pcount * feat, transcendentals=0
         ),
@@ -507,6 +554,13 @@
         refs.reshape(2, feat), particles, inv_sigma2.reshape(1, freqs), offsets.T, owner_map.reshape(1, slots),
         center.reshape(1, pcount),
     )
+    sums, loglik = pl.pallas_call(
+        last_kernel,
+        out_shape=(jax.ShapeDtypeStruct((2, 1, feat), F32), jax.ShapeDtypeStruct((1, pcount), F32)),
+        in_specs=[vmem, vmem],
+        out_specs=(vmem, vmem),
+        compiler_params=pltpu.CompilerParams(vmem_limit_bytes=grant),
+    )(partial, loglik)
     return sums, loglik.reshape(pcount)
 
 

time: 74.4 us -> 73 us (0.981)
  local copies, waits for them, and re-layouts: 2.8 us -> 0 us
  Pallas kernels: 70.9 us -> 72.2 us
    unnamed x2 -> x0, local copies, waits for them, and re-layouts: 2.8 us -> none
    pallas_call x0 -> x1, Pallas kernels: none -> 1.83 us  [per_device(): pl.pallas_call(last_kernel, out_shape=(jax.ShapeDtypeStruct((2, 1, feat),...]
where the time goes in v4:
time: 73 us; the launch traced here: 72.8 us
  Pallas kernels  72.2 us (99%)
    pallas_call x1, Pallas kernels, per_device(): pl.pallas_call(functools.partial(em_kernel, n_dom, n_ori, shifts), out_sh...  70.4 us
    pallas_call x1, Pallas kernels, per_device(): pl.pallas_call(last_kernel, out_shape=(jax.ShapeDtypeStruct((2, 1, feat),...  1.83 us

profile of v4, /device:TPU:2, one launch (start us, length us, event | category | flops | bytes accessed | tf_op | source)
XLA Modules:
  0.0 72.8 jit_solution(13240784962948512220)
XLA Ops:
  0.6 70.4 %shard_map.77 = (bf16[8,8,16,256]{3,2,1,0:T(8,128)(2,1)}, f32[1,256]{1,0:T(1,128)}) custom-call(bf16[2,16384]{1,0:T(2,128)(2,1)} %bitcast.6, bf16[256,16384]{1,0:T(8,128)(2,1)} %part_hbm.1, f32[1,8192]{1,0:T(1,128)} %bitcast.7, s32[2,9]{1,0:T(2,128)} %bitcast.8, s32[1,64]{1,0:T(1,128)} %bitcast.11, s32[1,256]{1,0:T(1,128)} %bitcast.9), custom_call_target="tpu_custom_call" | custom-call | flops 9663676416 | bytes 8388608 | tf_op jit(solution)/shard_map/pallas_call | solution.py:498
  71.0 1.8 %shard_map.78 = (f32[2,1,16384]{2,1,0:T(1,128)}, f32[1,256]{1,0:T(1,128)}) custom-call(bf16[8,8,16,256]{3,2,1,0:T(8,128)(2,1)} %get-tuple-element.6.recv2, f32[1,256]{1,0:T(1,128)} %get-tuple-element.7.loglik_in), custom_call_target="tpu_custom_call" | custom-call | tf_op jit(solution)/shard_map/pallas_call | solution.py:557

commit v5 on v4

--- a/solution.py
+++ b/solution.py
@@ -58,10 +58,6 @@
     return (a + by) % RING
 
 
-def tile_row(odd, h, k):
-    return pl.multiple_of((32 * h + 8 * k) * (1 - odd) + (16 * k + 8 * h) * odd, 8)
-
-
 def greet(barrier, to):
     pl.semaphore_signal(barrier, inc=1, device_id=to, device_id_type=MESH)
 
@@ -85,32 +81,27 @@
 
 
 def exchange(perm, perm_t):
-    for odd, ref, inverse in ((0, perm, 0), (1, perm, 0), (0, perm_t, 1), (1, perm_t, 1)):
-        there = lax.broadcasted_iota(jnp.int32, (256, 256), 0)
-        here = lax.broadcasted_iota(jnp.int32, (256, 256), 1)
-        out, src = (here, there) if inverse else (there, here)
-        at, s, q = src >> 4, (src >> 3) & 1, src & 7
-        if odd:
-            row = ((at >> 1) & 3) * 8 + (at >> 3) * 4 + (at & 1) * 2 + s
-        else:
-            row = at * 2 + s
-        ref[odd] = (out == q * 32 + row).astype(F32).astype(BF16)
+    there = lax.broadcasted_iota(jnp.int32, (128, 128), 0)
+    here = lax.broadcasted_iota(jnp.int32, (128, 128), 1)
+    for ref, out, src in ((perm, there, here), (perm_t, here, there)):
+        q, s, r = src >> 4, (src >> 3) & 1, src & 7
+        ref[...] = (out == r * 16 + q * 2 + s).astype(F32).astype(BF16)
 
 
 def em_kernel(
     n_dom, n_ori, shifts,
     refs_hbm, part_hbm, inv_hbm, off_hbm, omap_hbm, center_hbm,
     recv2, loglik_ref,
-    part, part_t, stage, mine, gath, rows, perm, perm_t, cos_tab, sin_tab, lhs_a, lhs_b, acc, prods_a, prods_b, power,
+    part, part_t, stage, mine, pieces, gath, perm, perm_t, cos_tab, sin_tab, lhs_a, lhs_b, acc, prods_a, prods_b, power,
     refs_ref, off_ref, inv_ref, omap_ref, center_ref, stat_out, stat_in, by_class, sends, far_in, near_in, send2,
-    part_sem, small_sem, ag_send, ag_recv, ag_near, ag_far, st_send, st_recv,
-    rs_send, far_sem, early_sem, late_sem, rs_recv,
+    part_sem, small_sem, ag_send, ag_recv, ring_send, ag_near, ag_far, st_send, st_recv,
+    rs_send, share_send, far_sem, early_sem, late_sem, rs_recv,
 ):
     freqs = inv_ref.shape[1]
     slots = 2 * n_dom
-    lanes = mine.shape[2]
+    lanes = mine.shape[3]
     width = freqs // CHUNKS
-    half = RING
+    half = 4
     here = Torus()
     axes, my_z = here.axes, here.z
     my_ori = lax.axis_index("orient")
@@ -145,41 +136,54 @@
                     at = r * freqs + c * width + g * lanes + j * 128
                     stage[j, pl.ds(c * 16 + r * GROUPS + g, 2, stride=8), :] = refs_ref[:, pl.ds(at, 128)].astype(F32)
         for j in range(lanes // 128):
-            mine[c, :, pl.ds(j * 128, 128)] = stage[j, pl.ds(c * 16, 16), :].astype(BF16)
+            mine[c % 2, c // 2, :, pl.ds(j * 128, 128)] = stage[j, pl.ds(c * 16, 16), :].astype(BF16)
 
     pl.semaphore_wait(barrier, len(peers) + n_ori - 1)
 
-    def gather0(c):
-        odd, v, u = axes(c)
-        home = u * 2 + my_z
-        at = v * 8 + home
-
-        def share(i, carry):
-            q = (home + i) % 8
-            send(mine.at[c], gath.at[c, at], ag_send.at[c], ag_recv.at[c], device(odd, v, q // 2, q % 2))
-            return carry
-
-        lax.fori_loop(1, 8, share, 0)
-        gath[c, at] = mine[c]
+    batches = ((0, 1), (1, 1), (2, PAIRS - 2))
+
+    def gather0(b):
+        for odd in range(2):
+            _, v, u = axes(0, odd)
+            home = u * 2 + my_z
+            ks = pl.ds(*batches[b])
+
+            def share(i, carry):
+                q = (home + i) % 8
+                send(
+                    mine.at[odd, ks], pieces.at[odd, home, ks], ag_send.at[b, odd], ag_recv.at[b, odd],
+                    device(odd, v, q // 2, q % 2),
+                )
+                return carry
+
+            lax.fori_loop(1, 8, share, 0)
+            pieces[odd, home, ks] = mine[odd, ks]
+
+    def gather0_wait(b):
+        for odd in range(2):
+            wait(pieces.at[odd, pl.ds(0, 7), pl.ds(*batches[b])], ag_recv.at[b, odd])
 
     def gather1(c):
         odd, v, u = axes(c)
-        wait(gath.at[c, pl.ds(0, 7)], ag_recv.at[c])
+        joined = jnp.dot(
+            perm[...], pieces[odd, :, c // 2].reshape(128, lanes), preferred_element_type=F32
+        ).astype(BF16)
+        gath[c, v] = joined.reshape(8, 16, lanes)
         for first in range(2):
             for k, by in ((0, 1), (1, 3)):
                 h = k if first == 0 else 1 - k
-                block = gath.at[c, pl.ds(v * 8 + h * half, half)]
-                send(block, block, ag_send.at[c], ag_near.at[c, k, h], device(odd, step(v, by), u, my_z))
+                block = gath.at[c, v, pl.ds(h * half, half)]
+                send(block, block, ring_send.at[c], ag_near.at[c, k, h], device(odd, step(v, by), u, my_z))
 
     def gather2(c):
         odd, v, u = axes(c)
         for k, by in ((0, 1), (1, 3)):
-            block = gath.at[c, pl.ds(step(v, 4 - by) * 8 + k * half, half)]
+            block = gath.at[c, step(v, 4 - by), pl.ds(k * half, half)]
             wait(block, ag_near.at[c, k, k])
-            send(block, block, ag_send.at[c], ag_far.at[c, k], device(odd, step(v, by), u, my_z))
+            send(block, block, ring_send.at[c], ag_far.at[c, k], device(odd, step(v, by), u, my_z))
 
     def gather3(c):
-        block = gath.at[c, pl.ds(0, half)]
+        block = gath.at[c, 0, pl.ds(0, half)]
         for k in range(2):
             wait(block, ag_near.at[c, k, 1 - k])
             wait(block, ag_far.at[c, k])
@@ -202,8 +206,8 @@
 
         lax.fori_loop(0, 8, turn, 0)
 
-    pair(0, gather0)
-    pair(1, gather0)
+    gather0(0)
+    gather0(1)
     exchange(perm, perm_t)
     smalls[1].wait()
 
@@ -227,14 +231,16 @@
         return carry
 
     lax.fori_loop(0, freqs // 1024, tables, 0)
+    gather0_wait(0)
     pair(0, gather1)
-    pair(2, gather0)
+    gather0(2)
     lax.fori_loop(freqs // 1024, freqs // 512, tables, 0)
+    gather0_wait(1)
     pair(1, gather1)
     turn_pair(0)
     pair(0, gather2)
-    pair(3, gather0)
     turn_pair(1)
+    gather0_wait(2)
     pair(2, gather1)
     for copy in smalls[2:]:
         copy.wait()
@@ -246,46 +252,39 @@
         at = pl.multiple_of(group * lanes, lanes)
         return pl.ds(at, lanes), pl.ds(pl.multiple_of(freqs + at, lanes), lanes)
 
-    def score_product(lhs, group):
-        block = jnp.concatenate([part_t[at, :] for at in columns(group)], axis=0)
-        acc[...] += jnp.dot(lhs[...], block, preferred_element_type=F32)
+    def score_product(lhs, c, half_chunk):
+        at = pl.multiple_of((2 * c + half_chunk) * 2 * lanes, 2 * lanes)
+        block = jnp.concatenate(
+            [part_t[pl.ds(at, 2 * lanes), :], part_t[pl.ds(pl.multiple_of(freqs + at, 2 * lanes), 2 * lanes), :]], axis=0
+        )
+        acc[c % 2] += jnp.dot(lhs[...], block, preferred_element_type=F32)
 
     def shift(lhs, c, g):
         for j in range(lanes // 128):
+            at = pl.ds(j * 128, 128)
+            col = g % 2 * lanes + j * 128
             there = pl.ds(pl.multiple_of((c * GROUPS + g) * lanes + j * 128, 128), 128)
-            real = rows[g, :, pl.ds(j * 128, 128)]
-            imag = rows[GROUPS + g, :, pl.ds(j * 128, 128)]
+            real = jnp.concatenate([gath[c, w, g, :, at] for w in range(RING)], axis=0).astype(F32)
+            imag = jnp.concatenate([gath[c, w, GROUPS + g, :, at] for w in range(RING)], axis=0).astype(F32)
             inv = inv_ref[:, there]
             re = real * inv
             im = imag * inv
-            power[...] += re * real + im * imag
+            power[c % 2] += re * real + im * imag
             for t in range(shifts):
                 cosine = cos_tab[pl.ds(t, 1), there]
                 sine = sin_tab[pl.ds(t, 1), there]
                 into = lhs.at[pl.ds(t * slots, slots)]
-                into[:, pl.ds(j * 128, 128)] = (re * cosine + im * sine).astype(BF16)
-                into[:, pl.ds(lanes + j * 128, 128)] = (im * cosine - re * sine).astype(BF16)
+                into[:, pl.ds(col, 128)] = (re * cosine + im * sine).astype(BF16)
+                into[:, pl.ds(2 * lanes + col, 128)] = (im * cosine - re * sine).astype(BF16)
 
     def score_chunk(c, carry):
-        odd = c % 2
         gather3(c)
-        for h in range(2):
-            spread = jnp.dot(
-                perm[odd], gath[c, pl.ds(16 * h, 16)].reshape(256, lanes), preferred_element_type=F32
-            )
-            for q in range(8):
-                for k in range(4):
-                    rows[q, pl.ds(tile_row(odd, h, k), 8), :] = spread[q * 32 + k * 8:q * 32 + k * 8 + 8, :]
-
-        def two_groups(i, carry):
-            first = c * GROUPS + 2 * i
-            score_product(lhs_b, jnp.maximum(first - 1, 0))
-            shift(lhs_a, c, 2 * i)
-            score_product(lhs_a, first)
-            shift(lhs_b, c, 2 * i + 1)
-            return carry
-
-        lax.fori_loop(0, GROUPS // 2, two_groups, 0)
+        score_product(lhs_b, jnp.maximum(c - 1, 0), 1)
+        shift(lhs_a, c, 0)
+        shift(lhs_a, c, 1)
+        score_product(lhs_a, c, 0)
+        shift(lhs_b, c, 2)
+        shift(lhs_b, c, 3)
 
         for k in range(PAIRS - 1):
             @pl.when(c == 2 * k)
@@ -304,21 +303,30 @@
         return carry
 
     lax.fori_loop(0, CHUNKS, score_chunk, 0)
-    score_product(lhs_b, CHUNKS * GROUPS - 1)
-
-    power_col = 0.5 * jnp.sum(power[...], axis=1, keepdims=True)
+    score_product(lhs_b, CHUNKS - 1, 1)
+
+    for base, ref in [(t * slots, acc) for t in range(shifts)] + [(0, power)]:
+        for y in range(4):
+            for x in range(4):
+                ref[0, pl.ds(base + y * 16 + x * 4, 4), :] += ref[1, pl.ds(base + x * 16 + y * 4, 4), :]
+
+    power_col = 0.5 * jnp.sum(power[0], axis=1, keepdims=True)
     distance = jnp.abs(my_ori - center_ref[...])
     allowed = jnp.minimum(distance, n_ori - distance) <= n_ori // 4
     best = None
     for t in range(shifts):
         at = pl.ds(t * slots, slots)
-        value = jnp.where(allowed, acc[at, :] - power_col, NEG_FILL)
-        acc[at, :] = value
+        value = jnp.where(allowed, acc[0, at, :] - power_col, NEG_FILL)
+        acc[0, at, :] = value
         top = jnp.max(value, axis=0, keepdims=True)
         best = top if best is None else jnp.maximum(best, top)
     total = jnp.zeros_like(best)
     for t in range(shifts):
-        total += jnp.sum(jnp.exp(acc[pl.ds(t * slots, slots), :] - best), axis=0, keepdims=True)
+        at = pl.ds(t * slots, slots)
+        value = jnp.exp(acc[0, at, :] - best)
+        acc[0, at, :] = value
+        total += jnp.sum(value, axis=0, keepdims=True)
+    mine_best = best
     stat_out[0:1, :] = best
     stat_out[1:2, :] = total
 
@@ -336,19 +344,27 @@
     best = functools.reduce(jnp.maximum, bests)
     total = sum(stat_in[o, 1:2, :] * jnp.exp(bests[o] - best) for o in range(n_ori))
     loglik_ref[...] = best + jnp.log(total)
+    scale = jnp.exp(mine_best - best) / total
 
     pick = (lax.broadcasted_iota(jnp.int32, (slots, slots), 0) == omap_ref[...]).astype(F32).astype(BF16)
     weights = jnp.concatenate(
-        [(jnp.exp(acc[pl.ds(t * slots, slots), :] - best) / total).astype(BF16) for t in range(shifts)], axis=1
+        [(acc[0, pl.ds(t * slots, slots), :] * scale).astype(BF16) for t in range(shifts)], axis=1
     )
-    picked = lax.dot_general(pick, weights, (((0,), (0,)), ((), ())), preferred_element_type=F32).astype(BF16)
-    pcount = acc.shape[1]
-    for t in range(shifts):
-        by_class[pl.ds(t * slots, slots), :] = picked[:, t * pcount:(t + 1) * pcount]
+    row = lax.broadcasted_iota(jnp.int32, (slots, slots), 1)
+    swapped = ((row >> 2) & 3) * 16 + (row >> 4) * 4 + (row & 3)
+    swap = (lax.broadcasted_iota(jnp.int32, (slots, slots), 0) == swapped).astype(F32).astype(BF16)
+    picks = jnp.concatenate([pick, jnp.dot(pick, swap, preferred_element_type=F32).astype(BF16)], axis=1)
+    picked = lax.dot_general(picks, weights, (((0,), (0,)), ((), ())), preferred_element_type=F32).astype(BF16)
+    pcount = acc.shape[2]
+    for odd in range(2):
+        for t in range(shifts):
+            by_class[odd, pl.ds(t * slots, slots), :] = picked[
+                odd * slots:(odd + 1) * slots, t * pcount:(t + 1) * pcount
+            ]
 
     def multiply(prods, group):
         block = jnp.concatenate([part[:, at] for at in columns(group)], axis=1)
-        prods[...] = jnp.dot(by_class[...], block, preferred_element_type=F32)
+        prods[...] = jnp.dot(by_class[group // GROUPS % 2], block, preferred_element_type=F32)
 
     def rotate(prods, c, g):
         for j in range(lanes // 128):
@@ -364,12 +380,11 @@
                 term_imag = im * cosine + re * sine
                 out_real = term_real if t == 0 else out_real + term_real
                 out_imag = term_imag if t == 0 else out_imag + term_imag
-            rows[g, :, at] = out_real
-            rows[GROUPS + g, :, at] = out_imag
+            for w in range(RING):
+                sends[c, w, g, :, at] = out_real[w * 16:(w + 1) * 16].astype(BF16)
+                sends[c, w, GROUPS + g, :, at] = out_imag[w * 16:(w + 1) * 16].astype(BF16)
 
     def sum_chunk(c):
-        odd = c % 2
-
         def two_groups(i, carry):
             first = c * GROUPS + 2 * i
             multiply(prods_b, first + 1)
@@ -379,40 +394,26 @@
             return carry
 
         lax.fori_loop(0, GROUPS // 2, two_groups, 0)
-        for h in range(2):
-            tiles = [rows[q, pl.ds(tile_row(odd, h, k), 8), :] for q in range(8) for k in range(4)]
-            spread = jnp.dot(
-                perm_t[odd], jnp.concatenate(tiles, axis=0).astype(BF16), preferred_element_type=F32
-            ).astype(BF16)
-            sends[c, pl.ds(16 * h, 16)] = spread.reshape(16, 16, lanes)
 
     def reduce0(c):
         odd, v, u = axes(c)
         for k, by in ((0, 1), (1, 3)):
             to = device(odd, step(v, by), u, my_z)
-            send(sends.at[c, pl.ds(step(v, 2) * 8 + k * half, half)], far_in.at[c, k], rs_send.at[c], far_sem.at[c, k], to)
+            send(sends.at[c, step(v, 2), pl.ds(k * half, half)], far_in.at[c, k], rs_send.at[c], far_sem.at[c, k], to)
         for k, by in ((0, 1), (1, 3)):
             to = device(odd, step(v, by), u, my_z)
-            other = (1 - k) * half
-            send(
-                sends.at[c, pl.ds(step(v, by) * 8 + other, half)], near_in.at[c, k, pl.ds(other, half)],
-                rs_send.at[c], early_sem.at[c, k], to,
-            )
+            other = pl.ds((1 - k) * half, half)
+            send(sends.at[c, step(v, by), other], near_in.at[c, k, other], rs_send.at[c], early_sem.at[c, k], to)
 
     def reduce1(c):
         odd, v, u = axes(c)
         for k, by in ((0, 1), (1, 3)):
             wait(far_in.at[c, k], far_sem.at[c, k])
-            at = step(v, by) * 8 + k * half
-
-            def add(i, carry):
-                sends[c, at + i] = (sends[c, at + i].astype(F32) + far_in[c, k, i].astype(F32)).astype(BF16)
-                return carry
-
-            lax.fori_loop(0, half, add, 0)
+            w, part_of = step(v, by), pl.ds(k * half, half)
+            sends[c, w, part_of] = (sends[c, w, part_of].astype(F32) + far_in[c, k].astype(F32)).astype(BF16)
             send(
-                sends.at[c, pl.ds(at, half)], near_in.at[c, k, pl.ds(k * half, half)], rs_send.at[c],
-                late_sem.at[c, k], device(odd, step(v, by), u, my_z),
+                sends.at[c, w, part_of], near_in.at[c, k, part_of], rs_send.at[c], late_sem.at[c, k],
+                device(odd, w, u, my_z),
             )
 
     def reduce2(c):
@@ -420,19 +421,16 @@
         for k in range(2):
             wait(near_in.at[c, k, pl.ds((1 - k) * half, half)], early_sem.at[c, k])
             wait(near_in.at[c, k, pl.ds(k * half, half)], late_sem.at[c, k])
-
-        def add(q, carry):
-            send2[c, q] = (
-                sends[c, v * 8 + q].astype(F32) + near_in[c, 0, q].astype(F32) + near_in[c, 1, q].astype(F32)
-            ).astype(BF16)
-            return carry
-
-        lax.fori_loop(0, 8, add, 0)
+        total = sends[c, v].astype(F32) + near_in[c, 0].astype(F32) + near_in[c, 1].astype(F32)
+        apart = jnp.dot(
+            perm_t[...], total.astype(BF16).reshape(128, lanes), preferred_element_type=F32
+        ).astype(BF16)
+        send2[c] = apart.reshape(8, 16, lanes)
         home = u * 2 + my_z
 
         def share(i, carry):
             q = (home + i) % 8
-            send(send2.at[c, q], recv2.at[c, home], rs_send.at[c], rs_recv.at[c], device(odd, v, q // 2, q % 2))
+            send(send2.at[c, q], recv2.at[c, home], share_send.at[c], rs_recv.at[c], device(odd, v, q // 2, q % 2))
             return carry
 
         lax.fori_loop(1, 8, share, 0)
@@ -459,10 +457,15 @@
     multiply(prods_a, 0)
     lax.fori_loop(0, CHUNKS + 2 * LAG, sum_step, 0)
 
+    for b in range(3):
+        for odd in range(2):
+            wait(pieces.at[odd, pl.ds(0, 7), pl.ds(*batches[b])], ag_send.at[b, odd])
+
     def drain(c, carry):
         wait(recv2.at[c, pl.ds(0, 7)], rs_recv.at[c])
-        wait(gath.at[c, pl.ds(0, n_dom - 1)], ag_send.at[c])
-        wait(sends.at[c, pl.ds(0, 31)], rs_send.at[c])
+        wait(gath.at[c, pl.ds(0, 3)], ring_send.at[c])
+        wait(sends.at[c, pl.ds(0, 3)], rs_send.at[c])
+        wait(send2.at[c, pl.ds(0, 7)], share_send.at[c])
         return carry
 
     lax.fori_loop(0, CHUNKS, drain, 0)
@@ -507,39 +510,41 @@
             pltpu.VMEM((pcount, feat), BF16),
             pltpu.VMEM((feat, pcount), BF16),
             pltpu.VMEM((lanes // 128, 16 * CHUNKS, 128), F32),
-            pltpu.VMEM((CHUNKS, 16, lanes), BF16),
-            pltpu.VMEM((CHUNKS, n_dom, 16, lanes), BF16),
-            pltpu.VMEM((2 * GROUPS, slots, lanes), F32),
-            pltpu.VMEM((2, 256, 256), BF16),
-            pltpu.VMEM((2, 256, 256), BF16),
+            pltpu.VMEM((2, PAIRS, 16, lanes), BF16),
+            pltpu.VMEM((2, 8, PAIRS, 16, lanes), BF16),
+            pltpu.VMEM((CHUNKS, RING, 8, 16, lanes), BF16),
+            pltpu.VMEM((128, 128), BF16),
+            pltpu.VMEM((128, 128), BF16),
             pltpu.VMEM((shifts, freqs), F32),
             pltpu.VMEM((shifts, freqs), F32),
-            pltpu.VMEM((shifts * slots, 2 * lanes), BF16),
-            pltpu.VMEM((shifts * slots, 2 * lanes), BF16),
-            pltpu.VMEM((shifts * slots, pcount), F32),
+            pltpu.VMEM((shifts * slots, 4 * lanes), BF16),
+            pltpu.VMEM((shifts * slots, 4 * lanes), BF16),
+            pltpu.VMEM((2, shifts * slots, pcount), F32),
             pltpu.VMEM((shifts * slots, 2 * lanes), F32),
             pltpu.VMEM((shifts * slots, 2 * lanes), F32),
-            pltpu.VMEM((slots, 128), F32),
+            pltpu.VMEM((2, slots, 128), F32),
             pltpu.VMEM((2, feat), BF16),
             pltpu.SMEM((2, shifts), jnp.int32),
             pltpu.VMEM((1, freqs), F32),
             pltpu.VMEM((1, slots), jnp.int32),
             pltpu.VMEM((1, pcount), jnp.int32),
-            pltpu.VMEM((8, pcount), F32),
-            pltpu.VMEM((n_ori, 8, pcount), F32),
-            pltpu.VMEM((shifts * slots, pcount), BF16),
-            pltpu.VMEM((CHUNKS, n_dom, 16, lanes), BF16),
-            pltpu.VMEM((CHUNKS, 2, RING, 16, lanes), BF16),
+            pltpu.VMEM((2, pcount), F32),
+            pltpu.VMEM((n_ori, 2, pcount), F32),
+            pltpu.VMEM((2, shifts * slots, pcount), BF16),
+            pltpu.VMEM((CHUNKS, RING, 8, 16, lanes), BF16),
+            pltpu.VMEM((CHUNKS, 2, 4, 16, lanes), BF16),
             pltpu.VMEM((CHUNKS, 2, 8, 16, lanes), BF16),
             pltpu.VMEM((CHUNKS, 8, 16, lanes), BF16),
             dma((CHUNKS,)),
             dma((5,)),
-            dma((CHUNKS,)),
+            dma((3, 2)),
+            dma((3, 2)),
             dma((CHUNKS,)),
             dma((CHUNKS, 2, 2)),
             dma((CHUNKS, 2)),
             dma,
             dma,
+            dma((CHUNKS,)),
             dma((CHUNKS,)),
             dma((CHUNKS, 2)),
             dma((CHUNKS, 2)),

time: 73 us -> 73.1 us (level)
  no operation moved by 1% of the time
where the time goes in v5:
time: 73.1 us; the launch traced here: 73 us
  Pallas kernels  72.4 us (99%)
    pallas_call x1, Pallas kernels, per_device(): pl.pallas_call(functools.partial(em_kernel, n_dom, n_ori, shifts), out_sh...  70.6 us
    pallas_call x1, Pallas kernels, per_device(): pl.pallas_call(last_kernel, out_shape=(jax.ShapeDtypeStruct((2, 1, feat),...  1.83 us

profile of v5, /device:TPU:2, one launch (start us, length us, event | category | flops | bytes accessed | tf_op | source)
XLA Modules:
  0.0 73.0 jit_solution(3885903397806107445)
XLA Ops:
  0.6 70.6 %shard_map.77 = (bf16[8,8,16,256]{3,2,1,0:T(8,128)(2,1)}, f32[1,256]{1,0:T(1,128)}) custom-call(bf16[2,16384]{1,0:T(2,128)(2,1)} %bitcast.6, bf16[256,16384]{1,0:T(8,128)(2,1)} %part_hbm.1, f32[1,8192]{1,0:T(1,128)} %bitcast.7, s32[2,9]{1,0:T(2,128)} %bitcast.8, s32[1,64]{1,0:T(1,128)} %bitcast.11, s32[1,256]{1,0:T(1,128)} %bitcast.9), custom_call_target="tpu_custom_call" | custom-call | flops 9663676416 | bytes 8388608 | tf_op jit(solution)/shard_map/pallas_call | solution.py:501
  71.2 1.8 %shard_map.78 = (f32[2,1,16384]{2,1,0:T(1,128)}, f32[1,256]{1,0:T(1,128)}) custom-call(bf16[8,8,16,256]{3,2,1,0:T(8,128)(2,1)} %get-tuple-element.6.recv2, f32[1,256]{1,0:T(1,128)} %get-tuple-element.7.loglik_in), custom_call_target="tpu_custom_call" | custom-call | tf_op jit(solution)/shard_map/pallas_call | solution.py:562

commit v6 on v5

--- a/solution.py
+++ b/solution.py
@@ -9,7 +9,7 @@
 from jax.sharding import PartitionSpec as P
 
 BOX = 128
-CHUNKS = 8
+CHUNKS = 4
 GROUPS = 4
 PAIRS = CHUNKS // 2
 LAG = CHUNKS // 4
@@ -140,7 +140,7 @@
 
     pl.semaphore_wait(barrier, len(peers) + n_ori - 1)
 
-    batches = ((0, 1), (1, 1), (2, PAIRS - 2))
+    batches = ((0, 1), (1, 1))
 
     def gather0(b):
         for odd in range(2):
@@ -233,15 +233,12 @@
     lax.fori_loop(0, freqs // 1024, tables, 0)
     gather0_wait(0)
     pair(0, gather1)
-    gather0(2)
     lax.fori_loop(freqs // 1024, freqs // 512, tables, 0)
     gather0_wait(1)
     pair(1, gather1)
     turn_pair(0)
     pair(0, gather2)
     turn_pair(1)
-    gather0_wait(2)
-    pair(2, gather1)
     for copy in smalls[2:]:
         copy.wait()
     acc[...] = jnp.zeros_like(acc)
@@ -286,19 +283,9 @@
         shift(lhs_b, c, 2)
         shift(lhs_b, c, 3)
 
-        for k in range(PAIRS - 1):
-            @pl.when(c == 2 * k)
-            def _():
-                pair(k + 1, gather2)
-
-        @pl.when(c == 1)
+        @pl.when(c == 0)
         def _():
-            pair(PAIRS - 1, gather1)
-
-        for k in range(2, PAIRS):
-            @pl.when(c == 2 * k - 3)
-            def _():
-                turn_pair(k)
+            pair(1, gather2)
 
         return carry
 
@@ -457,7 +444,7 @@
     multiply(prods_a, 0)
     lax.fori_loop(0, CHUNKS + 2 * LAG, sum_step, 0)
 
-    for b in range(3):
+    for b in range(2):
         for odd in range(2):
             wait(pieces.at[odd, pl.ds(0, 7), pl.ds(*batches[b])], ag_send.at[b, odd])
 
@@ -537,8 +524,8 @@
             pltpu.VMEM((CHUNKS, 8, 16, lanes), BF16),
             dma((CHUNKS,)),
             dma((5,)),
-            dma((3, 2)),
-            dma((3, 2)),
+            dma((2, 2)),
+            dma((2, 2)),
             dma((CHUNKS,)),
             dma((CHUNKS, 2, 2)),
             dma((CHUNKS, 2)),

time: 73.1 us -> 72.8 us (level)
  no operation moved by 1% of the time
where the time goes in v6:
time: 72.8 us; the launch traced here: 72.6 us
  Pallas kernels  71.9 us (99%)
    pallas_call x1, Pallas kernels, per_device(): pl.pallas_call(functools.partial(em_kernel, n_dom, n_ori, shifts), out_sh...  70.1 us
    pallas_call x1, Pallas kernels, per_device(): pl.pallas_call(last_kernel, out_shape=(jax.ShapeDtypeStruct((2, 1, feat),...  1.83 us

profile of v6, /device:TPU:2, one launch (start us, length us, event | category | flops | bytes accessed | tf_op | source)
XLA Modules:
  0.0 72.6 jit_solution(16463495652901750883)
XLA Ops:
  0.6 70.1 %shard_map.77 = (bf16[4,8,16,512]{3,2,1,0:T(8,128)(2,1)}, f32[1,256]{1,0:T(1,128)}) custom-call(bf16[2,16384]{1,0:T(2,128)(2,1)} %bitcast.6, bf16[256,16384]{1,0:T(8,128)(2,1)} %part_hbm.1, f32[1,8192]{1,0:T(1,128)} %bitcast.7, s32[2,9]{1,0:T(2,128)} %bitcast.8, s32[1,64]{1,0:T(1,128)} %bitcast.11, s32[1,256]{1,0:T(1,128)} %bitcast.9), custom_call_target="tpu_custom_call" | custom-call | flops 9663676416 | bytes 8388608 | tf_op jit(solution)/shard_map/pallas_call | solution.py:488
  70.7 1.8 %shard_map.78 = (f32[2,1,16384]{2,1,0:T(1,128)}, f32[1,256]{1,0:T(1,128)}) custom-call(bf16[4,8,16,512]{3,2,1,0:T(8,128)(2,1)} %get-tuple-element.6.recv2, f32[1,256]{1,0:T(1,128)} %get-tuple-element.7.loglik_in), custom_call_target="tpu_custom_call" | custom-call | tf_op jit(solution)/shard_map/pallas_call | solution.py:549

commit v7 on v6

--- a/solution.py
+++ b/solution.py
@@ -12,7 +12,6 @@
 CHUNKS = 4
 GROUPS = 4
 PAIRS = CHUNKS // 2
-LAG = CHUNKS // 4
 RING = 4
 NEG_FILL = -1e30
 MESH = pl.DeviceIdType.MESH
@@ -134,7 +133,7 @@
             for g in range(GROUPS):
                 for j in range(lanes // 128):
                     at = r * freqs + c * width + g * lanes + j * 128
-                    stage[j, pl.ds(c * 16 + r * GROUPS + g, 2, stride=8), :] = refs_ref[:, pl.ds(at, 128)].astype(F32)
+                    stage[j, pl.ds(c * 16 + g * 2 + r, 2, stride=8), :] = refs_ref[:, pl.ds(at, 128)].astype(F32)
         for j in range(lanes // 128):
             mine[c % 2, c // 2, :, pl.ds(j * 128, 128)] = stage[j, pl.ds(c * 16, 16), :].astype(BF16)
 
@@ -182,11 +181,10 @@
             wait(block, ag_near.at[c, k, k])
             send(block, block, ring_send.at[c], ag_far.at[c, k], device(odd, step(v, by), u, my_z))
 
-    def gather3(c):
+    def gather3(c, h):
         block = gath.at[c, 0, pl.ds(0, half)]
-        for k in range(2):
-            wait(block, ag_near.at[c, k, 1 - k])
-            wait(block, ag_far.at[c, k])
+        wait(block, ag_near.at[c, 1 - h, h])
+        wait(block, ag_far.at[c, h])
 
     def pair(k, stage):
         def one(i, carry):
@@ -254,15 +252,17 @@
         block = jnp.concatenate(
             [part_t[pl.ds(at, 2 * lanes), :], part_t[pl.ds(pl.multiple_of(freqs + at, 2 * lanes), 2 * lanes), :]], axis=0
         )
-        acc[c % 2] += jnp.dot(lhs[...], block, preferred_element_type=F32)
+        for m in range(0, shifts * slots, shifts * slots // 2):
+            rows = pl.ds(m, shifts * slots // 2)
+            acc[c % 2, rows, :] += jnp.dot(lhs[rows, :], block, preferred_element_type=F32)
 
     def shift(lhs, c, g):
         for j in range(lanes // 128):
             at = pl.ds(j * 128, 128)
             col = g % 2 * lanes + j * 128
             there = pl.ds(pl.multiple_of((c * GROUPS + g) * lanes + j * 128, 128), 128)
-            real = jnp.concatenate([gath[c, w, g, :, at] for w in range(RING)], axis=0).astype(F32)
-            imag = jnp.concatenate([gath[c, w, GROUPS + g, :, at] for w in range(RING)], axis=0).astype(F32)
+            real = jnp.concatenate([gath[c, w, 2 * g, :, at] for w in range(RING)], axis=0).astype(F32)
+            imag = jnp.concatenate([gath[c, w, 2 * g + 1, :, at] for w in range(RING)], axis=0).astype(F32)
             inv = inv_ref[:, there]
             re = real * inv
             im = imag * inv
@@ -275,10 +275,11 @@
                 into[:, pl.ds(2 * lanes + col, 128)] = (im * cosine - re * sine).astype(BF16)
 
     def score_chunk(c, carry):
-        gather3(c)
+        gather3(c, 0)
         score_product(lhs_b, jnp.maximum(c - 1, 0), 1)
         shift(lhs_a, c, 0)
         shift(lhs_a, c, 1)
+        gather3(c, 1)
         score_product(lhs_a, c, 0)
         shift(lhs_b, c, 2)
         shift(lhs_b, c, 3)
@@ -368,33 +369,31 @@
                 out_real = term_real if t == 0 else out_real + term_real
                 out_imag = term_imag if t == 0 else out_imag + term_imag
             for w in range(RING):
-                sends[c, w, g, :, at] = out_real[w * 16:(w + 1) * 16].astype(BF16)
-                sends[c, w, GROUPS + g, :, at] = out_imag[w * 16:(w + 1) * 16].astype(BF16)
-
-    def sum_chunk(c):
-        def two_groups(i, carry):
-            first = c * GROUPS + 2 * i
-            multiply(prods_b, first + 1)
-            rotate(prods_a, c, 2 * i)
-            multiply(prods_a, jnp.minimum(first + 2, CHUNKS * GROUPS - 1))
-            rotate(prods_b, c, 2 * i + 1)
-            return carry
-
-        lax.fori_loop(0, GROUPS // 2, two_groups, 0)
-
-    def reduce0(c):
+                sends[c, w, 2 * g, :, at] = out_real[w * 16:(w + 1) * 16].astype(BF16)
+                sends[c, w, 2 * g + 1, :, at] = out_imag[w * 16:(w + 1) * 16].astype(BF16)
+
+    def sum_half(c, h):
+        first = c * GROUPS + 2 * h
+        multiply(prods_b, first + 1)
+        rotate(prods_a, c, 2 * h)
+        multiply(prods_a, jnp.minimum(first + 2, CHUNKS * GROUPS - 1))
+        rotate(prods_b, c, 2 * h + 1)
+
+    def reduce0(c, h):
         odd, v, u = axes(c)
-        for k, by in ((0, 1), (1, 3)):
-            to = device(odd, step(v, by), u, my_z)
-            send(sends.at[c, step(v, 2), pl.ds(k * half, half)], far_in.at[c, k], rs_send.at[c], far_sem.at[c, k], to)
-        for k, by in ((0, 1), (1, 3)):
-            to = device(odd, step(v, by), u, my_z)
-            other = pl.ds((1 - k) * half, half)
-            send(sends.at[c, step(v, by), other], near_in.at[c, k, other], rs_send.at[c], early_sem.at[c, k], to)
-
-    def reduce1(c):
+        part_of = pl.ds(h * half, half)
+        to = device(odd, step(v, 1 + 2 * h), u, my_z)
+        send(sends.at[c, step(v, 2), part_of], far_in.at[c, h], rs_send.at[c], far_sem.at[c, h], to)
+        w = step(v, 3 - 2 * h)
+        send(
+            sends.at[c, w, part_of], near_in.at[c, 1 - h, part_of], rs_send.at[c], early_sem.at[c, 1 - h],
+            device(odd, w, u, my_z),
+        )
+
+    def reduce1(c, ks):
         odd, v, u = axes(c)
-        for k, by in ((0, 1), (1, 3)):
+        for k in ks:
+            by = 1 + 2 * k
             wait(far_in.at[c, k], far_sem.at[c, k])
             w, part_of = step(v, by), pl.ds(k * half, half)
             sends[c, w, part_of] = (sends[c, w, part_of].astype(F32) + far_in[c, k].astype(F32)).astype(BF16)
@@ -423,26 +422,26 @@
         lax.fori_loop(1, 8, share, 0)
         recv2[c, home] = send2[c, home]
 
-    def progress(c):
-        @pl.when((c >= LAG) & (c < CHUNKS + LAG))
+    def sum_step(i, carry):
+        c, h = i // 2, i % 2
+        sum_half(c, h)
+        reduce0(c, h)
+        for k in range(2):
+            @pl.when((h == k) & (c >= 1))
+            def _():
+                reduce1(c - 1, (k,))
+
+        @pl.when((h == 1) & (c >= 2))
         def _():
-            reduce1(c - LAG)
-
-        @pl.when(c >= 2 * LAG)
-        def _():
-            reduce2(c - 2 * LAG)
-
-    def sum_step(c, carry):
-        @pl.when(c < CHUNKS)
-        def _():
-            sum_chunk(c)
-            reduce0(c)
-
-        progress(c)
+            reduce2(c - 2)
+
         return carry
 
     multiply(prods_a, 0)
-    lax.fori_loop(0, CHUNKS + 2 * LAG, sum_step, 0)
+    lax.fori_loop(0, 2 * CHUNKS, sum_step, 0)
+    reduce1(CHUNKS - 1, (0, 1))
+    reduce2(CHUNKS - 2)
+    reduce2(CHUNKS - 1)
 
     for b in range(2):
         for odd in range(2):
@@ -470,7 +469,7 @@
             for s in range(2):
                 for r in range(2):
                     for g in range(GROUPS):
-                        row = s * 8 + r * GROUPS + g
+                        row = s * 8 + g * 2 + r
                         at = r * freqs + c * GROUPS * lanes + g * lanes + j * 128
                         out_ref[s, :, pl.ds(at, 128)] = total[row:row + 1, :]
 

time: 72.8 us -> 72.4 us (level)
  no operation moved by 1% of the time
where the time goes in v7:
time: 72.4 us; the launch traced here: 72.3 us
  Pallas kernels  71.7 us (99%)
    pallas_call x1, Pallas kernels, per_device(): pl.pallas_call(functools.partial(em_kernel, n_dom, n_ori, shifts), out_sh...  69.8 us
    pallas_call x1, Pallas kernels, per_device(): pl.pallas_call(last_kernel, out_shape=(jax.ShapeDtypeStruct((2, 1, feat),...  1.83 us

profile of v7, /device:TPU:2, one launch (start us, length us, event | category | flops | bytes accessed | tf_op | source)
XLA Modules:
  0.0 72.3 jit_solution(7792266383750274902)
XLA Ops:
  0.6 69.8 %shard_map.77 = (bf16[4,8,16,512]{3,2,1,0:T(8,128)(2,1)}, f32[1,256]{1,0:T(1,128)}) custom-call(bf16[2,16384]{1,0:T(2,128)(2,1)} %bitcast.6, bf16[256,16384]{1,0:T(8,128)(2,1)} %part_hbm.1, f32[1,8192]{1,0:T(1,128)} %bitcast.7, s32[2,9]{1,0:T(2,128)} %bitcast.8, s32[1,64]{1,0:T(1,128)} %bitcast.11, s32[1,256]{1,0:T(1,128)} %bitcast.9), custom_call_target="tpu_custom_call" | custom-call | flops 9663676416 | bytes 8388608 | tf_op jit(solution)/shard_map/pallas_call | solution.py:487
  70.5 1.8 %shard_map.78 = (f32[2,1,16384]{2,1,0:T(1,128)}, f32[1,256]{1,0:T(1,128)}) custom-call(bf16[4,8,16,512]{3,2,1,0:T(8,128)(2,1)} %get-tuple-element.6.recv2, f32[1,256]{1,0:T(1,128)} %get-tuple-element.7.loglik_in), custom_call_target="tpu_custom_call" | custom-call | tf_op jit(solution)/shard_map/pallas_call | solution.py:548

commit v8 on v7

--- a/solution.py
+++ b/solution.py
@@ -34,10 +34,14 @@
 class Torus:
     def __init__(self):
         self.me = lax.axis_index("dom")
+        self.core = lax.axis_index("orient") % 2
         self.y, self.x, self.z = self.me // 8, (self.me // 2) % 4, self.me % 2
 
-    def axes(self, c, odd=None):
-        odd = c % 2 if odd is None else odd
+    def turned(self, c):
+        return (c + self.core) % 2
+
+    def axes(self, c):
+        odd = self.turned(c)
         return odd, self.y * (1 - odd) + self.x * odd, self.x * (1 - odd) + self.y * odd
 
     def peers(self):
@@ -71,12 +75,11 @@
     pltpu.make_async_copy(ref, ref, sem).wait()
 
 
-def fetch_particles(part_hbm, part, part_sem, freqs):
+def fetch_particles(part_hbm, part, part_sem, freqs, c):
     width = freqs // CHUNKS
-    for c in range(CHUNKS):
-        for base in (0, freqs):
-            cols = pl.ds(base + c * width, width)
-            pltpu.make_async_copy(part_hbm.at[:, cols], part.at[:, cols], part_sem.at[c]).start()
+    for base in (0, freqs):
+        cols = pl.ds(base + c * width, width)
+        pltpu.make_async_copy(part_hbm.at[:, cols], part.at[:, cols], part_sem.at[c]).start()
 
 
 def exchange(perm, perm_t):
@@ -102,7 +105,7 @@
     width = freqs // CHUNKS
     half = 4
     here = Torus()
-    axes, my_z = here.axes, here.z
+    axes, turned, my_z = here.axes, here.turned, here.z
     my_ori = lax.axis_index("orient")
 
     smalls = [
@@ -125,7 +128,6 @@
         return carry
 
     lax.fori_loop(1, n_ori, greet_ori, 0)
-    fetch_particles(part_hbm, part, part_sem, freqs)
     smalls[0].wait()
 
     for c in range(CHUNKS):
@@ -142,30 +144,30 @@
     batches = ((0, 1), (1, 1))
 
     def gather0(b):
-        for odd in range(2):
-            _, v, u = axes(0, odd)
+        for kind in range(2):
+            odd, v, u = axes(kind)
             home = u * 2 + my_z
             ks = pl.ds(*batches[b])
 
             def share(i, carry):
                 q = (home + i) % 8
                 send(
-                    mine.at[odd, ks], pieces.at[odd, home, ks], ag_send.at[b, odd], ag_recv.at[b, odd],
+                    mine.at[kind, ks], pieces.at[kind, home, ks], ag_send.at[b, kind], ag_recv.at[b, kind],
                     device(odd, v, q // 2, q % 2),
                 )
                 return carry
 
             lax.fori_loop(1, 8, share, 0)
-            pieces[odd, home, ks] = mine[odd, ks]
+            pieces[kind, home, ks] = mine[kind, ks]
 
     def gather0_wait(b):
-        for odd in range(2):
-            wait(pieces.at[odd, pl.ds(0, 7), pl.ds(*batches[b])], ag_recv.at[b, odd])
+        for kind in range(2):
+            wait(pieces.at[kind, pl.ds(0, 7), pl.ds(*batches[b])], ag_recv.at[b, kind])
 
     def gather1(c):
         odd, v, u = axes(c)
         joined = jnp.dot(
-            perm[...], pieces[odd, :, c // 2].reshape(128, lanes), preferred_element_type=F32
+            perm[...], pieces[c % 2, :, c // 2].reshape(128, lanes), preferred_element_type=F32
         ).astype(BF16)
         gath[c, v] = joined.reshape(8, 16, lanes)
         for first in range(2):
@@ -206,6 +208,8 @@
 
     gather0(0)
     gather0(1)
+    for c in range(2):
+        fetch_particles(part_hbm, part, part_sem, freqs, c)
     exchange(perm, perm_t)
     smalls[1].wait()
 
@@ -234,6 +238,8 @@
     lax.fori_loop(freqs // 1024, freqs // 512, tables, 0)
     gather0_wait(1)
     pair(1, gather1)
+    for c in range(2, CHUNKS):
+        fetch_particles(part_hbm, part, part_sem, freqs, c)
     turn_pair(0)
     pair(0, gather2)
     turn_pair(1)
@@ -254,7 +260,7 @@
         )
         for m in range(0, shifts * slots, shifts * slots // 2):
             rows = pl.ds(m, shifts * slots // 2)
-            acc[c % 2, rows, :] += jnp.dot(lhs[rows, :], block, preferred_element_type=F32)
+            acc[turned(c), rows, :] += jnp.dot(lhs[rows, :], block, preferred_element_type=F32)
 
     def shift(lhs, c, g):
         for j in range(lanes // 128):
@@ -266,7 +272,7 @@
             inv = inv_ref[:, there]
             re = real * inv
             im = imag * inv
-            power[c % 2] += re * real + im * imag
+            power[turned(c)] += re * real + im * imag
             for t in range(shifts):
                 cosine = cos_tab[pl.ds(t, 1), there]
                 sine = sin_tab[pl.ds(t, 1), there]
@@ -352,7 +358,7 @@
 
     def multiply(prods, group):
         block = jnp.concatenate([part[:, at] for at in columns(group)], axis=1)
-        prods[...] = jnp.dot(by_class[group // GROUPS % 2], block, preferred_element_type=F32)
+        prods[...] = jnp.dot(by_class[turned(group // GROUPS)], block, preferred_element_type=F32)
 
     def rotate(prods, c, g):
         for j in range(lanes // 128):

time: 72.4 us -> 72.5 us (level)
  no operation moved by 1% of the time
where the time goes in v8:
time: 72.5 us; the launch traced here: 72.2 us
  Pallas kernels  71.6 us (99%)
    pallas_call x1, Pallas kernels, per_device(): pl.pallas_call(functools.partial(em_kernel, n_dom, n_ori, shifts), out_sh...  69.7 us
    pallas_call x1, Pallas kernels, per_device(): pl.pallas_call(last_kernel, out_shape=(jax.ShapeDtypeStruct((2, 1, feat),...  1.83 us

profile of v8, /device:TPU:2, one launch (start us, length us, event | category | flops | bytes accessed | tf_op | source)
XLA Modules:
  0.0 72.2 jit_solution(12163108916694827105)
XLA Ops:
  0.6 69.7 %shard_map.77 = (bf16[4,8,16,512]{3,2,1,0:T(8,128)(2,1)}, f32[1,256]{1,0:T(1,128)}) custom-call(bf16[2,16384]{1,0:T(2,128)(2,1)} %bitcast.6, bf16[256,16384]{1,0:T(8,128)(2,1)} %part_hbm.1, f32[1,8192]{1,0:T(1,128)} %bitcast.7, s32[2,9]{1,0:T(2,128)} %bitcast.8, s32[1,64]{1,0:T(1,128)} %bitcast.11, s32[1,256]{1,0:T(1,128)} %bitcast.9), custom_call_target="tpu_custom_call" | custom-call | flops 9663676416 | bytes 8388608 | tf_op jit(solution)/shard_map/pallas_call | solution.py:493
  70.4 1.8 %shard_map.78 = (f32[2,1,16384]{2,1,0:T(1,128)}, f32[1,256]{1,0:T(1,128)}) custom-call(bf16[4,8,16,512]{3,2,1,0:T(8,128)(2,1)} %get-tuple-element.6.recv2, f32[1,256]{1,0:T(1,128)} %get-tuple-element.7.loglik_in), custom_call_target="tpu_custom_call" | custom-call | tf_op jit(solution)/shard_map/pallas_call | solution.py:554

commit v9 on v8

--- a/solution.py
+++ b/solution.py
@@ -95,9 +95,9 @@
     refs_hbm, part_hbm, inv_hbm, off_hbm, omap_hbm, center_hbm,
     recv2, loglik_ref,
     part, part_t, stage, mine, pieces, gath, perm, perm_t, cos_tab, sin_tab, lhs_a, lhs_b, acc, prods_a, prods_b, power,
-    refs_ref, off_ref, inv_ref, omap_ref, center_ref, stat_out, stat_in, by_class, sends, far_in, near_in, send2,
-    part_sem, small_sem, ag_send, ag_recv, ring_send, ag_near, ag_far, st_send, st_recv,
-    rs_send, share_send, far_sem, early_sem, late_sem, rs_recv,
+    refs_ref, off_ref, inv_ref, omap_ref, center_ref, stat_out, stat_in, by_class, sends, near_in, send2,
+    part_sem, small_sem, ag_send, ag_recv, ring_send, ag_ring, st_send, st_recv,
+    rs_send, share_send, near_sem, rs_recv,
 ):
     freqs = inv_ref.shape[1]
     slots = 2 * n_dom
@@ -170,23 +170,13 @@
             perm[...], pieces[c % 2, :, c // 2].reshape(128, lanes), preferred_element_type=F32
         ).astype(BF16)
         gath[c, v] = joined.reshape(8, 16, lanes)
-        for first in range(2):
-            for k, by in ((0, 1), (1, 3)):
-                h = k if first == 0 else 1 - k
-                block = gath.at[c, v, pl.ds(h * half, half)]
-                send(block, block, ring_send.at[c], ag_near.at[c, k, h], device(odd, step(v, by), u, my_z))
-
-    def gather2(c):
-        odd, v, u = axes(c)
-        for k, by in ((0, 1), (1, 3)):
-            block = gath.at[c, step(v, 4 - by), pl.ds(k * half, half)]
-            wait(block, ag_near.at[c, k, k])
-            send(block, block, ring_send.at[c], ag_far.at[c, k], device(odd, step(v, by), u, my_z))
-
-    def gather3(c, h):
-        block = gath.at[c, 0, pl.ds(0, half)]
-        wait(block, ag_near.at[c, 1 - h, h])
-        wait(block, ag_far.at[c, h])
+        for h in range(2):
+            block = gath.at[c, v, pl.ds(h * half, half)]
+            for by in (2, 1, 3):
+                send(block, block, ring_send.at[c], ag_ring.at[c, h], device(odd, step(v, by), u, my_z))
+
+    def gather2(c, h):
+        wait(gath.at[c, pl.ds(0, RING - 1), pl.ds(h * half, half)], ag_ring.at[c, h])
 
     def pair(k, stage):
         def one(i, carry):
@@ -241,7 +231,6 @@
     for c in range(2, CHUNKS):
         fetch_particles(part_hbm, part, part_sem, freqs, c)
     turn_pair(0)
-    pair(0, gather2)
     turn_pair(1)
     for copy in smalls[2:]:
         copy.wait()
@@ -281,18 +270,14 @@
                 into[:, pl.ds(2 * lanes + col, 128)] = (im * cosine - re * sine).astype(BF16)
 
     def score_chunk(c, carry):
-        gather3(c, 0)
+        gather2(c, 0)
         score_product(lhs_b, jnp.maximum(c - 1, 0), 1)
         shift(lhs_a, c, 0)
         shift(lhs_a, c, 1)
-        gather3(c, 1)
+        gather2(c, 1)
         score_product(lhs_a, c, 0)
         shift(lhs_b, c, 2)
         shift(lhs_b, c, 3)
-
-        @pl.when(c == 0)
-        def _():
-            pair(1, gather2)
 
         return carry
 
@@ -388,32 +373,19 @@
     def reduce0(c, h):
         odd, v, u = axes(c)
         part_of = pl.ds(h * half, half)
-        to = device(odd, step(v, 1 + 2 * h), u, my_z)
-        send(sends.at[c, step(v, 2), part_of], far_in.at[c, h], rs_send.at[c], far_sem.at[c, h], to)
-        w = step(v, 3 - 2 * h)
-        send(
-            sends.at[c, w, part_of], near_in.at[c, 1 - h, part_of], rs_send.at[c], early_sem.at[c, 1 - h],
-            device(odd, w, u, my_z),
-        )
-
-    def reduce1(c, ks):
-        odd, v, u = axes(c)
-        for k in ks:
-            by = 1 + 2 * k
-            wait(far_in.at[c, k], far_sem.at[c, k])
-            w, part_of = step(v, by), pl.ds(k * half, half)
-            sends[c, w, part_of] = (sends[c, w, part_of].astype(F32) + far_in[c, k].astype(F32)).astype(BF16)
+        for by in (2, 1, 3):
+            w = step(v, by)
             send(
-                sends.at[c, w, part_of], near_in.at[c, k, part_of], rs_send.at[c], late_sem.at[c, k],
+                sends.at[c, w, part_of], near_in.at[c, by - 1, part_of], rs_send.at[c], near_sem.at[c],
                 device(odd, w, u, my_z),
             )
 
-    def reduce2(c):
+    def reduce1(c):
         odd, v, u = axes(c)
-        for k in range(2):
-            wait(near_in.at[c, k, pl.ds((1 - k) * half, half)], early_sem.at[c, k])
-            wait(near_in.at[c, k, pl.ds(k * half, half)], late_sem.at[c, k])
-        total = sends[c, v].astype(F32) + near_in[c, 0].astype(F32) + near_in[c, 1].astype(F32)
+        wait(near_in.at[c], near_sem.at[c])
+        total = sends[c, v].astype(F32)
+        for k in range(RING - 1):
+            total += near_in[c, k].astype(F32)
         apart = jnp.dot(
             perm_t[...], total.astype(BF16).reshape(128, lanes), preferred_element_type=F32
         ).astype(BF16)
@@ -432,22 +404,16 @@
         c, h = i // 2, i % 2
         sum_half(c, h)
         reduce0(c, h)
-        for k in range(2):
-            @pl.when((h == k) & (c >= 1))
-            def _():
-                reduce1(c - 1, (k,))
-
-        @pl.when((h == 1) & (c >= 2))
+
+        @pl.when((h == 1) & (c >= 1))
         def _():
-            reduce2(c - 2)
+            reduce1(c - 1)
 
         return carry
 
     multiply(prods_a, 0)
     lax.fori_loop(0, 2 * CHUNKS, sum_step, 0)
-    reduce1(CHUNKS - 1, (0, 1))
-    reduce2(CHUNKS - 2)
-    reduce2(CHUNKS - 1)
+    reduce1(CHUNKS - 1)
 
     for b in range(2):
         for odd in range(2):
@@ -524,23 +490,19 @@
             pltpu.VMEM((n_ori, 2, pcount), F32),
             pltpu.VMEM((2, shifts * slots, pcount), BF16),
             pltpu.VMEM((CHUNKS, RING, 8, 16, lanes), BF16),
-            pltpu.VMEM((CHUNKS, 2, 4, 16, lanes), BF16),
-            pltpu.VMEM((CHUNKS, 2, 8, 16, lanes), BF16),
+            pltpu.VMEM((CHUNKS, RING - 1, 8, 16, lanes), BF16),
             pltpu.VMEM((CHUNKS, 8, 16, lanes), BF16),
             dma((CHUNKS,)),
             dma((5,)),
             dma((2, 2)),
             dma((2, 2)),
             dma((CHUNKS,)),
-            dma((CHUNKS, 2, 2)),
             dma((CHUNKS, 2)),
             dma,
             dma,
             dma((CHUNKS,)),
             dma((CHUNKS,)),
-            dma((CHUNKS, 2)),
-            dma((CHUNKS, 2)),
-            dma((CHUNKS, 2)),
+            dma((CHUNKS,)),
             dma((CHUNKS,)),
         ],
         compiler_params=pltpu.CompilerParams(collective_id=0, has_side_effects=True, vmem_limit_bytes=grant),

time: 72.5 us -> 70.5 us (0.972)
  Pallas kernels: 71.6 us -> 69.2 us
    pallas_call x1, Pallas kernels: 69.7 us -> 67.3 us  [per_device(): pl.pallas_call(functools.partial(em_kernel, n_dom, n_ori, shifts), out_sh...]
where the time goes in v9:
time: 70.5 us; the launch traced here: 69.8 us
  Pallas kernels  69.2 us (98%)
    pallas_call x1, Pallas kernels, per_device(): pl.pallas_call(functools.partial(em_kernel, n_dom, n_ori, shifts), out_sh...  67.3 us
    pallas_call x1, Pallas kernels, per_device(): pl.pallas_call(last_kernel, out_shape=(jax.ShapeDtypeStruct((2, 1, feat),...  1.83 us

profile of v9, /device:TPU:2, one launch (start us, length us, event | category | flops | bytes accessed | tf_op | source)
XLA Modules:
  0.0 69.8 jit_solution(2285840079564948923)
XLA Ops:
  0.6 67.3 %shard_map.77 = (bf16[4,8,16,512]{3,2,1,0:T(8,128)(2,1)}, f32[1,256]{1,0:T(1,128)}) custom-call(bf16[2,16384]{1,0:T(2,128)(2,1)} %bitcast.6, bf16[256,16384]{1,0:T(8,128)(2,1)} %part_hbm.1, f32[1,8192]{1,0:T(1,128)} %bitcast.7, s32[2,9]{1,0:T(2,128)} %bitcast.8, s32[1,64]{1,0:T(1,128)} %bitcast.11, s32[1,256]{1,0:T(1,128)} %bitcast.9), custom_call_target="tpu_custom_call" | custom-call | flops 9663676416 | bytes 8388608 | tf_op jit(solution)/shard_map/pallas_call | solution.py:459
  68.0 1.8 %shard_map.78 = (f32[2,1,16384]{2,1,0:T(1,128)}, f32[1,256]{1,0:T(1,128)}) custom-call(bf16[4,8,16,512]{3,2,1,0:T(8,128)(2,1)} %get-tuple-element.6.recv2, f32[1,256]{1,0:T(1,128)} %get-tuple-element.7.loglik_in), custom_call_target="tpu_custom_call" | custom-call | tf_op jit(solution)/shard_map/pallas_call | solution.py:516

commit v10 on v9

--- a/solution.py
+++ b/solution.py
@@ -231,7 +231,6 @@
     for c in range(2, CHUNKS):
         fetch_particles(part_hbm, part, part_sem, freqs, c)
     turn_pair(0)
-    turn_pair(1)
     for copy in smalls[2:]:
         copy.wait()
     acc[...] = jnp.zeros_like(acc)
@@ -270,14 +269,18 @@
                 into[:, pl.ds(2 * lanes + col, 128)] = (im * cosine - re * sine).astype(BF16)
 
     def score_chunk(c, carry):
+        score_product(lhs_b, jnp.maximum(c - 1, 0), 1)
         gather2(c, 0)
-        score_product(lhs_b, jnp.maximum(c - 1, 0), 1)
         shift(lhs_a, c, 0)
         shift(lhs_a, c, 1)
+        score_product(lhs_a, c, 0)
         gather2(c, 1)
-        score_product(lhs_a, c, 0)
         shift(lhs_b, c, 2)
         shift(lhs_b, c, 3)
+
+        @pl.when(c == 1)
+        def _():
+            turn_pair(1)
 
         return carry
 
@@ -315,6 +318,11 @@
 
     lax.fori_loop(1, n_ori, stat_send, 0)
     stat_in[my_ori] = stat_out[...]
+    pick = (lax.broadcasted_iota(jnp.int32, (slots, slots), 0) == omap_ref[...]).astype(F32).astype(BF16)
+    row = lax.broadcasted_iota(jnp.int32, (slots, slots), 1)
+    swapped = ((row >> 2) & 3) * 16 + (row >> 4) * 4 + (row & 3)
+    swap = (lax.broadcasted_iota(jnp.int32, (slots, slots), 0) == swapped).astype(F32).astype(BF16)
+    picks = jnp.concatenate([pick, jnp.dot(pick, swap, preferred_element_type=F32).astype(BF16)], axis=1)
     if n_ori > 1:
         others = stat_in.at[pl.ds(0, n_ori - 1)]
         wait(others, st_recv)
@@ -325,14 +333,9 @@
     loglik_ref[...] = best + jnp.log(total)
     scale = jnp.exp(mine_best - best) / total
 
-    pick = (lax.broadcasted_iota(jnp.int32, (slots, slots), 0) == omap_ref[...]).astype(F32).astype(BF16)
     weights = jnp.concatenate(
         [(acc[0, pl.ds(t * slots, slots), :] * scale).astype(BF16) for t in range(shifts)], axis=1
     )
-    row = lax.broadcasted_iota(jnp.int32, (slots, slots), 1)
-    swapped = ((row >> 2) & 3) * 16 + (row >> 4) * 4 + (row & 3)
-    swap = (lax.broadcasted_iota(jnp.int32, (slots, slots), 0) == swapped).astype(F32).astype(BF16)
-    picks = jnp.concatenate([pick, jnp.dot(pick, swap, preferred_element_type=F32).astype(BF16)], axis=1)
     picked = lax.dot_general(picks, weights, (((0,), (0,)), ((), ())), preferred_element_type=F32).astype(BF16)
     pcount = acc.shape[2]
     for odd in range(2):

time: 70.5 us -> 70.2 us (level)
  no operation moved by 1% of the time
where the time goes in v10:
time: 70.2 us; the launch traced here: 69.4 us
  Pallas kernels  68.8 us (98%)
    pallas_call x1, Pallas kernels, per_device(): pl.pallas_call(functools.partial(em_kernel, n_dom, n_ori, shifts), out_sh...  67 us
    pallas_call x1, Pallas kernels, per_device(): pl.pallas_call(last_kernel, out_shape=(jax.ShapeDtypeStruct((2, 1, feat),...  1.83 us

profile of v10, /device:TPU:2, one launch (start us, length us, event | category | flops | bytes accessed | tf_op | source)
XLA Modules:
  0.0 69.4 jit_solution(1842374439388809472)
XLA Ops:
  0.6 67.0 %shard_map.77 = (bf16[4,8,16,512]{3,2,1,0:T(8,128)(2,1)}, f32[1,256]{1,0:T(1,128)}) custom-call(bf16[2,16384]{1,0:T(2,128)(2,1)} %bitcast.6, bf16[256,16384]{1,0:T(8,128)(2,1)} %part_hbm.1, f32[1,8192]{1,0:T(1,128)} %bitcast.7, s32[2,9]{1,0:T(2,128)} %bitcast.8, s32[1,64]{1,0:T(1,128)} %bitcast.11, s32[1,256]{1,0:T(1,128)} %bitcast.9), custom_call_target="tpu_custom_call" | custom-call | flops 9663676416 | bytes 8388608 | tf_op jit(solution)/shard_map/pallas_call | solution.py:462
  67.6 1.8 %shard_map.78 = (f32[2,1,16384]{2,1,0:T(1,128)}, f32[1,256]{1,0:T(1,128)}) custom-call(bf16[4,8,16,512]{3,2,1,0:T(8,128)(2,1)} %get-tuple-element.6.recv2, f32[1,256]{1,0:T(1,128)} %get-tuple-element.7.loglik_in), custom_call_target="tpu_custom_call" | custom-call | tf_op jit(solution)/shard_map/pallas_call | solution.py:519

commit v11 on v10

--- a/solution.py
+++ b/solution.py
@@ -94,7 +94,7 @@
     n_dom, n_ori, shifts,
     refs_hbm, part_hbm, inv_hbm, off_hbm, omap_hbm, center_hbm,
     recv2, loglik_ref,
-    part, part_t, stage, mine, pieces, gath, perm, perm_t, cos_tab, sin_tab, lhs_a, lhs_b, acc, prods_a, prods_b, power,
+    part, stage, mine, pieces, gath, perm, perm_t, cos_tab, sin_tab, lhs_a, lhs_b, acc, prods_a, prods_b, power,
     refs_ref, off_ref, inv_ref, omap_ref, center_ref, stat_out, stat_in, by_class, sends, near_in, send2,
     part_sem, small_sem, ag_send, ag_recv, ring_send, ag_ring, st_send, st_recv,
     rs_send, share_send, near_sem, rs_recv,
@@ -185,17 +185,6 @@
 
         lax.fori_loop(0, 2, one, 0)
 
-    def turn_pair(k):
-        for c in (2 * k, 2 * k + 1):
-            wait(part.at[:, pl.ds(0, 2 * width)], part_sem.at[c])
-
-        def turn(i, carry):
-            at = pl.ds(pl.multiple_of(i // 4 * freqs + k * 2 * width + i % 4 * (width // 2), width // 2), width // 2)
-            part_t[at, :] = part[:, at].T
-            return carry
-
-        lax.fori_loop(0, 8, turn, 0)
-
     gather0(0)
     gather0(1)
     for c in range(2):
@@ -230,7 +219,6 @@
     pair(1, gather1)
     for c in range(2, CHUNKS):
         fetch_particles(part_hbm, part, part_sem, freqs, c)
-    turn_pair(0)
     for copy in smalls[2:]:
         copy.wait()
     acc[...] = jnp.zeros_like(acc)
@@ -244,11 +232,13 @@
     def score_product(lhs, c, half_chunk):
         at = pl.multiple_of((2 * c + half_chunk) * 2 * lanes, 2 * lanes)
         block = jnp.concatenate(
-            [part_t[pl.ds(at, 2 * lanes), :], part_t[pl.ds(pl.multiple_of(freqs + at, 2 * lanes), 2 * lanes), :]], axis=0
+            [part[:, pl.ds(at, 2 * lanes)], part[:, pl.ds(pl.multiple_of(freqs + at, 2 * lanes), 2 * lanes)]], axis=1
         )
         for m in range(0, shifts * slots, shifts * slots // 2):
             rows = pl.ds(m, shifts * slots // 2)
-            acc[turned(c), rows, :] += jnp.dot(lhs[rows, :], block, preferred_element_type=F32)
+            acc[turned(c), rows, :] += lax.dot_general(
+                lhs[rows, :], block, (((1,), (1,)), ((), ())), preferred_element_type=F32
+            )
 
     def shift(lhs, c, g):
         for j in range(lanes // 128):
@@ -269,6 +259,7 @@
                 into[:, pl.ds(2 * lanes + col, 128)] = (im * cosine - re * sine).astype(BF16)
 
     def score_chunk(c, carry):
+        wait(part.at[:, pl.ds(0, 2 * width)], part_sem.at[c])
         score_product(lhs_b, jnp.maximum(c - 1, 0), 1)
         gather2(c, 0)
         shift(lhs_a, c, 0)
@@ -277,10 +268,6 @@
         gather2(c, 1)
         shift(lhs_b, c, 2)
         shift(lhs_b, c, 3)
-
-        @pl.when(c == 1)
-        def _():
-            turn_pair(1)
 
         return carry
 
@@ -323,6 +310,11 @@
     swapped = ((row >> 2) & 3) * 16 + (row >> 4) * 4 + (row & 3)
     swap = (lax.broadcasted_iota(jnp.int32, (slots, slots), 0) == swapped).astype(F32).astype(BF16)
     picks = jnp.concatenate([pick, jnp.dot(pick, swap, preferred_element_type=F32).astype(BF16)], axis=1)
+    for b in range(2):
+        for kind in range(2):
+            wait(pieces.at[kind, pl.ds(0, 7), pl.ds(*batches[b])], ag_send.at[b, kind])
+    for c in range(CHUNKS):
+        wait(gath.at[c, pl.ds(0, RING - 1)], ring_send.at[c])
     if n_ori > 1:
         others = stat_in.at[pl.ds(0, n_ori - 1)]
         wait(others, st_recv)
@@ -416,20 +408,14 @@
 
     multiply(prods_a, 0)
     lax.fori_loop(0, 2 * CHUNKS, sum_step, 0)
+    for c in range(CHUNKS - 1):
+        wait(sends.at[c, pl.ds(0, RING - 1)], rs_send.at[c])
     reduce1(CHUNKS - 1)
 
-    for b in range(2):
-        for odd in range(2):
-            wait(pieces.at[odd, pl.ds(0, 7), pl.ds(*batches[b])], ag_send.at[b, odd])
-
-    def drain(c, carry):
+    wait(sends.at[CHUNKS - 1, pl.ds(0, RING - 1)], rs_send.at[CHUNKS - 1])
+    for c in range(CHUNKS):
+        wait(send2.at[c, pl.ds(0, 7)], share_send.at[c])
         wait(recv2.at[c, pl.ds(0, 7)], rs_recv.at[c])
-        wait(gath.at[c, pl.ds(0, 3)], ring_send.at[c])
-        wait(sends.at[c, pl.ds(0, 3)], rs_send.at[c])
-        wait(send2.at[c, pl.ds(0, 7)], share_send.at[c])
-        return carry
-
-    lax.fori_loop(0, CHUNKS, drain, 0)
 
 
 def last_kernel(recv2, loglik_in, out_ref, loglik_ref):
@@ -469,7 +455,6 @@
         out_specs=(vmem, vmem),
         scratch_shapes=[
             pltpu.VMEM((pcount, feat), BF16),
-            pltpu.VMEM((feat, pcount), BF16),
             pltpu.VMEM((lanes // 128, 16 * CHUNKS, 128), F32),
             pltpu.VMEM((2, PAIRS, 16, lanes), BF16),
             pltpu.VMEM((2, 8, PAIRS, 16, lanes), BF16),

time: 70.2 us -> 69 us (0.983)
  Pallas kernels: 68.8 us -> 67.6 us
    pallas_call x1, Pallas kernels: 67 us -> 65.8 us  [per_device(): pl.pallas_call(functools.partial(em_kernel, n_dom, n_ori, shifts), out_sh...]
where the time goes in v11:
time: 69 us; the launch traced here: 68.3 us
  Pallas kernels  67.6 us (98%)
    pallas_call x1, Pallas kernels, per_device(): pl.pallas_call(functools.partial(em_kernel, n_dom, n_ori, shifts), out_sh...  65.8 us
    pallas_call x1, Pallas kernels, per_device(): pl.pallas_call(last_kernel, out_shape=(jax.ShapeDtypeStruct((2, 1, feat),...  1.83 us

profile of v11, /device:TPU:2, one launch (start us, length us, event | category | flops | bytes accessed | tf_op | source)
XLA Modules:
  0.0 68.3 jit_solution(13964137469640530531)
XLA Ops:
  0.6 65.8 %shard_map.77 = (bf16[4,8,16,512]{3,2,1,0:T(8,128)(2,1)}, f32[1,256]{1,0:T(1,128)}) custom-call(bf16[2,16384]{1,0:T(2,128)(2,1)} %bitcast.6, bf16[256,16384]{1,0:T(8,128)(2,1)} %part_hbm.1, f32[1,8192]{1,0:T(1,128)} %bitcast.7, s32[2,9]{1,0:T(2,128)} %bitcast.8, s32[1,64]{1,0:T(1,128)} %bitcast.11, s32[1,256]{1,0:T(1,128)} %bitcast.9), custom_call_target="tpu_custom_call" | custom-call | flops 9663676416 | bytes 8388608 | tf_op jit(solution)/shard_map/pallas_call | solution.py:448
  66.5 1.8 %shard_map.78 = (f32[2,1,16384]{2,1,0:T(1,128)}, f32[1,256]{1,0:T(1,128)}) custom-call(bf16[4,8,16,512]{3,2,1,0:T(8,128)(2,1)} %get-tuple-element.6.recv2, f32[1,256]{1,0:T(1,128)} %get-tuple-element.7.loglik_in), custom_call_target="tpu_custom_call" | custom-call | tf_op jit(solution)/shard_map/pallas_call | solution.py:504
